TPU v7x, 128 devices: a whole 4x4x4 slice. The times are simulated.
128 devices in a mesh: dp: 32 (over z, y, x_hi), mp: 2 (over x_lo), grid: 2 (over core).
Axes of the slice: x: 4 (x_hi: 2, x_lo: 2; x = x_hi * 2 + x_lo), y: 4, z: 4, core: 2. Of those that a mesh axis runs over, the one named last changes fastest.
Arguments:
- tokens: bfloat16 [16384, 768], P(('dp', 'grid')), may hold values from -6 to 6
- seq_lengths: int32 [32], P('dp'), may hold values from 257 to 512, as said below
- cotangent: bfloat16 [16384, 768], P(('dp', 'grid')), may hold values from -6 to 6
- qkv_weight: bfloat16 [3, 768, 768], P(None, 'mp'), may hold values from -0.21875 to 0.21875
- qv_bias: float32 [2, 768], P(None, 'mp'), may hold values from -1.2 to 1.2
- out_weight: bfloat16 [768, 768], P('mp'), may hold values from -0.875 to 0.875
- out_bias: float32 [768], replicated, may hold values from -2 to 2
- first_gain: float32 [768], replicated, may hold values from 0.5 to 1.5
- first_shift: float32 [768], replicated, may hold values from -2 to 2
- second_gain: float32 [768], replicated, may hold values from 0.5 to 1.5
- second_shift: float32 [768], replicated, may hold values from -2 to 2
- up_weight: bfloat16 [768, 3072], P('mp', 'grid'), may hold values from -0.21875 to 0.21875
- up_bias: float32 [3072], P('grid'), may hold values from -3 to 3
- down_weight: bfloat16 [768, 3072], P('mp', 'grid'), may hold values from -0.21875 to 0.21875
- down_bias: float32 [768], P('mp'), may hold values from -2 to 2
Outputs:
- layer_out: bfloat16 [16384, 768], P(('dp', 'grid'), 'mp')
- input_grad: float32 [16384, 768], P(('dp', 'grid'))
- grad_qkv_weight: float32 [3, 768, 768], P(None, 'mp')
- grad_qv_bias: float32 [2, 768], P(None, 'mp')
- grad_out_weight: float32 [768, 768], P('mp')
- grad_out_bias: float32 [768], replicated
- grad_first_gain: float32 [768], replicated
- grad_first_shift: float32 [768], replicated
- grad_second_gain: float32 [768], replicated
- grad_second_shift: float32 [768], replicated
- grad_up_weight: float32 [768, 3072], P('mp', 'grid')
- grad_up_bias: float32 [3072], P('grid')
- grad_down_weight: float32 [768, 3072], P('mp', 'grid')
- grad_down_bias: float32 [768], P('mp')
Inputs may be any that keep to these rules, and one draw needn't show every extreme that they name: Group g holds one sequence in its first seq_lengths[g] rows; every later row of the group is a padding row that sees only itself. Some group is full in every draw.
All inputs are finite; a program needn't handle non-finite values.
Results may differ from a plain program's by a relative error of at most 0.0085.
Values may be sent and summed in bfloat16 or wider, within the bound.
A program may use at most 128 MiB of HBM per device.

v0:
```python
import jax
import jax.numpy as jnp
from jax import lax
from jax.sharding import PartitionSpec as P

HD = 64


EPS = 1e-05
NEG = -1e30


def layer_norm(values, gain, shift):
    mean_row = jnp.mean(values, axis=-1, keepdims=True)
    centred = values - mean_row
    spread = jnp.mean(centred * centred, axis=-1, keepdims=True)
    return centred * lax.rsqrt(spread + EPS) * gain + shift


def gelu_tanh(values):
    return jax.nn.gelu(values, approximate=True)


def visible(query_pos, key_pos, length):
    same_row = key_pos[None, :] == query_pos[:, None]
    earlier = (key_pos[None, :] < query_pos[:, None]) & (query_pos[:, None] < length)
    return same_row | earlier


def contract_rows(left, right):
    return lax.dot_general(
        left, right, (((0,), (0,)), ((), ())), preferred_element_type=jnp.float32
    )


def contract_cols(left, right):
    return lax.dot_general(
        left, right, (((1,), (1,)), ((), ())), preferred_element_type=jnp.float32
    )


def sum_mlp(grads):
    return lax.psum((grads[0], grads[1], grads[2], grads[3]), "dp")


def per_device(
    tokens,
    seq_lengths,
    cotangent,
    qkv_weight,
    qv_bias,
    out_weight,
    out_bias,
    first_gain,
    first_shift,
    second_gain,
    second_shift,
    up_weight,
    up_bias,
    down_weight,
    down_bias,
):
    f32 = jnp.float32
    bf16 = jnp.bfloat16
    row_count, full_width = tokens.shape
    grid_count = lax.axis_size("grid")
    model_count = lax.axis_size("mp")
    group_rows = row_count * grid_count
    local_width = qkv_weight.shape[1]
    heads_here = local_width // HD
    score_scale = HD ** (-0.5)
    block_rows = min(512, group_rows)
    grid_pos = lax.axis_index("grid")
    model_pos = lax.axis_index("mp")
    length = seq_lengths[0]
    query_pos = grid_pos * row_count + jnp.arange(row_count, dtype=jnp.int32)
    last_block = (grid_pos * row_count + row_count - 1) // block_rows + 1
    inputs = tokens.astype(f32)
    normed1 = layer_norm(inputs, first_gain, first_shift).astype(bf16)
    queries = (contract_cols(normed1, qkv_weight[0]) + qv_bias[0]).astype(bf16)
    keys_here = contract_cols(normed1, qkv_weight[1]).astype(bf16)
    values_here = (contract_cols(normed1, qkv_weight[2]) + qv_bias[1]).astype(bf16)
    keys_all, values_all = (
        lax.all_gather(keys_here, "grid", axis=0, tiled=True),
        lax.all_gather(values_here, "grid", axis=0, tiled=True),
    )
    query_heads = queries.reshape(row_count, heads_here, HD)
    key_heads = keys_all.reshape(group_rows, heads_here, HD)
    value_heads = values_all.reshape(group_rows, heads_here, HD)

    def key_block(block_index):
        first_row = block_index * block_rows
        key_pos = first_row + jnp.arange(block_rows, dtype=jnp.int32)
        scores = (
            jnp.einsum("qhd,khd->hqk", query_heads, key_heads, preferred_element_type=f32)
            * score_scale
        )
        allowed = visible(query_pos, key_pos, length)[None]
        return (key_heads, value_heads, scores, allowed)

    def stats_step(block_index, state_in):
        row_max, row_sum = state_in
        key_piece, value_piece, scores, allowed = key_block(block_index)
        scores = jnp.where(allowed, scores, NEG)
        new_max = jnp.maximum(row_max, jnp.max(scores, axis=-1))
        expd = jnp.where(allowed, jnp.exp(scores - new_max[..., None]), 0.0)
        row_sum = row_sum * jnp.exp(row_max - new_max) + jnp.sum(expd, axis=-1)
        return (new_max, row_sum)

    start_max = jnp.full((heads_here, row_count), NEG, f32)
    start_sum = jnp.zeros((heads_here, row_count), f32)
    row_max, row_sum = lax.fori_loop(0, last_block, stats_step, (start_max, start_sum))
    log_total = row_max + jnp.log(row_sum)

    def output_step(block_index, accum):
        key_piece, value_piece, scores, allowed = key_block(block_index)
        probs_low = jnp.where(allowed, jnp.exp(scores - log_total[..., None]), 0.0).astype(bf16)
        return accum + jnp.einsum(
            "hqk,khd->qhd", probs_low, value_piece, preferred_element_type=f32
        )

    attended = lax.fori_loop(
        0, last_block, output_step, jnp.zeros((row_count, heads_here, HD), f32)
    )
    attended = attended.reshape(row_count, local_width)
    attended_low = attended.astype(bf16)
    branch = lax.psum(jnp.dot(attended_low, out_weight, preferred_element_type=f32), "mp")
    hidden1 = inputs + branch + out_bias
    normed2_full = layer_norm(hidden1, second_gain, second_shift).astype(bf16)
    part_width = full_width // model_count
    col_start = model_pos * part_width
    hidden1_part = lax.dynamic_slice_in_dim(hidden1, col_start, part_width, 1)
    normed2 = lax.dynamic_slice_in_dim(normed2_full, col_start, part_width, 1)
    grad_part = lax.dynamic_slice_in_dim(cotangent, col_start, part_width, 1)
    normed2_all, grad_all = (
        lax.all_gather(normed2, "grid", axis=0, tiled=True),
        lax.all_gather(grad_part, "grid", axis=0, tiled=True),
    )
    piece = normed2_all
    pre_act = (
        lax.psum_scatter(
            jnp.dot(piece, up_weight, preferred_element_type=f32),
            "mp",
            scatter_dimension=0,
            tiled=True,
        )
        + up_bias
    )
    activated, gelu_back = jax.vjp(gelu_tanh, pre_act)
    hidden = activated.astype(bf16)
    hidden_all = lax.all_gather(hidden, "mp", axis=0, tiled=True)
    piece = hidden_all
    mlp_out = lax.psum_scatter(
        contract_cols(piece, down_weight), "grid", scatter_dimension=0, tiled=True
    )
    layer_out = (hidden1_part + mlp_out + down_bias).astype(bf16)
    grad_down = contract_rows(grad_all, hidden_all)
    grad_down_bias = jnp.sum(grad_all.astype(f32), axis=0)
    piece = grad_all
    grad_act = lax.psum_scatter(
        jnp.dot(piece, down_weight, preferred_element_type=f32),
        "mp",
        scatter_dimension=0,
        tiled=True,
    )
    grad_pre = gelu_back(grad_act)[0].astype(bf16)
    grad_pre_all = lax.all_gather(grad_pre, "mp", axis=0, tiled=True)
    grad_up = contract_rows(normed2_all, grad_pre_all)
    grad_up_bias = jnp.sum(grad_pre_all.astype(f32), axis=0)
    piece = grad_pre_all
    grad_normed2 = lax.psum_scatter(
        contract_cols(piece, up_weight), "grid", scatter_dimension=0, tiled=True
    )
    mlp_grads = (grad_up, grad_up_bias, grad_down, grad_down_bias)
    grad_normed2_full = lax.all_gather(grad_normed2, "mp", axis=1, tiled=True)
    _, second_back = jax.vjp(layer_norm, hidden1, second_gain, second_shift)
    grad_h1_norm, grad_second_gain, grad_second_shift = second_back(grad_normed2_full)
    grad_hidden1 = cotangent.astype(f32) + grad_h1_norm
    grad_branch = grad_hidden1.astype(bf16)
    grad_out_weight = contract_rows(attended_low, grad_branch)
    grad_out_bias = jnp.sum(grad_branch.astype(f32), axis=0)
    grad_attended = contract_cols(grad_branch, out_weight).astype(bf16)
    grad_heads = grad_attended.reshape(row_count, heads_here, HD)
    delta = jnp.einsum(
        "qhd,qhd->hq", grad_heads.astype(f32), attended.reshape(row_count, heads_here, HD)
    )

    def grad_step(block_index, state_in):
        grad_query_acc, grad_keys_acc, grad_values_acc = state_in
        key_piece, value_piece, scores, allowed = key_block(block_index)
        probs_full = jnp.where(allowed, jnp.exp(scores - log_total[..., None]), 0.0)
        grad_probs = jnp.einsum("qhd,khd->hqk", grad_heads, value_piece, preferred_element_type=f32)
        grad_scores = (probs_full * (grad_probs - delta[..., None])).astype(bf16)
        grad_query_acc = grad_query_acc + jnp.einsum(
            "hqk,khd->qhd", grad_scores, key_piece, preferred_element_type=f32
        )
        key_grad_block = (
            jnp.einsum("hqk,qhd->khd", grad_scores, query_heads, preferred_element_type=f32)
            * score_scale
        )
        value_grad_block = jnp.einsum(
            "hqk,qhd->khd", probs_full.astype(bf16), grad_heads, preferred_element_type=f32
        )
        first_row = block_index * block_rows
        grad_keys_acc = key_grad_block
        grad_values_acc = value_grad_block
        return (grad_query_acc, grad_keys_acc, grad_values_acc)

    zero_query = jnp.zeros((row_count, heads_here, HD), f32)
    zero_keys = jnp.zeros((group_rows, heads_here, HD), f32)
    grad_query_acc, grad_keys_acc, grad_values_acc = lax.fori_loop(
        0, last_block, grad_step, (zero_query, zero_keys, zero_keys)
    )
    grad_keys_sum, grad_values_sum = (
        lax.psum_scatter(
            grad_keys_acc.reshape(group_rows, local_width), "grid", scatter_dimension=0, tiled=True
        ),
        lax.psum_scatter(
            grad_values_acc.reshape(group_rows, local_width),
            "grid",
            scatter_dimension=0,
            tiled=True,
        ),
    )
    grad_query = (grad_query_acc * score_scale).reshape(row_count, local_width).astype(bf16)
    grad_keys = grad_keys_sum.astype(bf16)
    grad_values = grad_values_sum.astype(bf16)
    grad_qkv_weight = jnp.stack(
        [
            contract_rows(grad_query, normed1),
            contract_rows(grad_keys, normed1),
            contract_rows(grad_values, normed1),
        ]
    )
    grad_qv_bias = jnp.stack(
        [jnp.sum(grad_query.astype(f32), axis=0), jnp.sum(grad_values.astype(f32), axis=0)]
    )
    grad_normed1_part = (
        jnp.dot(grad_query, qkv_weight[0], preferred_element_type=f32)
        + jnp.dot(grad_keys, qkv_weight[1], preferred_element_type=f32)
        + jnp.dot(grad_values, qkv_weight[2], preferred_element_type=f32)
    )
    grad_normed1 = lax.psum(grad_normed1_part, "mp")
    _, first_back = jax.vjp(layer_norm, inputs, first_gain, first_shift)
    grad_x_norm, grad_first_gain, grad_first_shift = first_back(grad_normed1)
    input_grad = grad_hidden1 + grad_x_norm
    attn_grads = lax.psum(
        (
            grad_qkv_weight,
            grad_qv_bias,
            grad_out_weight,
            grad_out_bias,
            grad_first_gain,
            grad_first_shift,
            grad_second_gain,
            grad_second_shift,
        ),
        ("dp", "grid"),
    )
    mlp_grads = sum_mlp(mlp_grads)
    return (
        layer_out,
        input_grad,
        attn_grads[0],
        attn_grads[1],
        attn_grads[2],
        attn_grads[3],
        attn_grads[4],
        attn_grads[5],
        attn_grads[6],
        attn_grads[7],
        mlp_grads[0],
        mlp_grads[1],
        mlp_grads[2],
        mlp_grads[3],
    )


def solution(mesh):
    placed = (
        P(("dp", "grid"), None),
        P("dp"),
        P(("dp", "grid"), None),
        P(None, "mp", None),
        P(None, "mp"),
        P("mp", None),
        P(),
        P(),
        P(),
        P(),
        P(),
        P("mp", "grid"),
        P("grid"),
        P("mp", "grid"),
        P("mp"),
    )
    return jax.shard_map(
        per_device,
        mesh=mesh,
        in_specs=placed,
        out_specs=(
            P(("dp", "grid"), "mp"),
            P(("dp", "grid"), None),
            P(None, "mp", None),
            P(None, "mp"),
            P("mp", None),
            P(),
            P(),
            P(),
            P(),
            P(),
            P("mp", "grid"),
            P("grid"),
            P("mp", "grid"),
            P("mp"),
        ),
        check_vma=False,
    )
```

profile of v0, /device:TPU:1, one launch (start us, length us, event | category | flops | bytes accessed | tf_op | source)
XLA Modules:
  0.0 1409.4 jit_solution(6379325593234282796)
XLA Ops:
  7.3 1.2 convert_reduce_fusion.1
  8.5 1.2 fusion.48
  9.8 0.8 slice_reduce_fusion
  10.6 1.7 convolution_convert_fusion.1
  12.3 1.5 fusion.42
  13.8 3.1 all_gather.22
  16.9 1.0 copy.38
  17.9 1.5 fusion.41
  19.5 2.1 all_gather.21
  21.8 1.1 copy.39
  22.9 1.7 copy.40
  24.6 2.9 while.39
  25.5 0.8 fusion.151
  26.3 1.1 select_reduce_fusion.2
  28.1 3.6 while.40
  29.1 2.7 fusion.155
  32.5 1.3 fusion.88
  33.9 2.1 all_gather.25
  36.0 3.9 fusion.91
  40.7 36.3 %all-reduce.9.cloned.1.call-done = f32[256,768]{1,0:T(8,128)} async-done(((f32[256,768]{1,0:T(8,128)}), f32[256,768]{1,0:T(8,128)}) %all-reduce.9.cloned.1.call-update) | async-done | bytes 786448 | tf_op jit(solution)/shard_map/psum | solution.py:127
  77.0 1.3 fusion.85
  78.8 2.4 all_gather.23
  81.9 2.6 fusion.89
  84.7 42.2 %reduce-scatter.11.cloned.1.call-done = f32[256,1536]{1,0:T(8,128)} async-done(((f32[512,1536]{1,0:T(8,128)}), f32[256,1536]{1,0:T(8,128)}) %reduce-scatter.11.cloned.1.call-update) | async-done | bytes 1572880 | tf_op jit(solution)/shard_map/reduce_scatter | solution.py:160
  126.9 49.2 %reduce-scatter.7.cloned.1.call-done = f32[256,1536]{1,0:T(8,128)} async-done(((f32[512,1536]{1,0:T(8,128)}), f32[256,1536]{1,0:T(8,128)}) %reduce-scatter.7.cloned.1.call-update) | async-done | bytes 1572880 | tf_op jit(solution)/shard_map/reduce_scatter | solution.py:141
  176.1 4.2 fusion.36
  180.4 30.8 %all-gather.5.cloned.1.call-done = bf16[512,1536]{1,0:T(8,128)(2,1)} async-done(((bf16[256,1536]{1,0:T(8,128)(2,1)}), bf16[512,1536]{1,0:T(8,128)(2,1)}) %all-gather.5.cloned.1.call-update) | async-done | bytes 1572880 | tf_op jit(solution)/shard_map/all_gather | solution.py:167
  211.2 3.3 fusion.92
  215.1 11.9 reduce-scatter.13.cloned.1.call-done
  227.0 11.7 all_gather.27
  238.8 0.9 fusion.81
  240.7 0.8 convert_reduce_fusion.3
  241.9 0.8 copy.41
  242.7 1.8 fusion.67
  244.5 1.0 broadcast_in_dim.74.clone
  245.5 1.0 broadcast_in_dim.74
  246.5 8.0 while.41
  248.0 2.5 fusion.169
  250.5 2.1 multiply_convert_fusion.5
  253.2 1.3 fusion.168
  255.3 4.5 all-gather.3.cloned.1.call-done
  259.7 3.6 fusion.90
  264.2 2.3 fusion.55
  266.5 8.6 reduce-scatter.15.cloned.1.call-done
  275.0 2.7 convolution_add_fusion.1
  277.8 12.6 reduce-scatter.17.cloned.1.call-done
  290.4 2.7 convolution_add_fusion
  293.2 3.7 fusion.95
  296.9 2.2 fusion.94
  300.2 1.3 fusion.93
  302.5 2.0 pad_maximum_fusion
  304.7 1.7 convert_reduce_fusion
  306.4 159.2 %all-reduce.2 = (f32[1536]{0:T(1024)}, f32[384]{0:T(512)}) all-reduce(f32[1536]{0:T(1024)S(1)} %convert_reduce_fusion, f32[384]{0:T(512)S(1)} %convert_reduce_fusion.2), channel_id=1, replica_groups=mesh['dp'=32,'mp'=2,'grid'=2] {'dp'}, use_global_device_ids=true, to_apply=%region_41.42 | all-reduce | flops 1920 | bytes 15360 | tf_op jit(solution)/shard_map/psum | solution.py:43
  465.7 1.7 add_convert_fusion
  467.7 1.5 fusion.82
  469.7 344.6 %all-reduce = (f32[2,384]{1,0:T(2,128)}, f32[768]{0:T(1024)}, f32[768]{0:T(1024)}, f32[768]{0:T(1024)}, f32[768]{0:T(1024)}, /*index=5*/f32[768]{0:T(1024)}) all-reduce(f32[2,384]{1,0:T(2,128)S(1)} %pad_maximum_fusion.1, f32[768]{0:T(1024)S(1)} %copy-done.30, ...), channel_id=1, replica_groups=mesh['dp'=32,'mp'=2,'grid'=2] {'dp','grid'}, use_global_device_ids=true, to_apply=%region_27.28 | all-reduce | flops 4608 | bytes 36864 | tf_op jit(solution)/shard_map/psum | solution.py:247
  814.3 1.3 add_add_fusion.2
  815.5 576.9 %all-reduce.13.cloned.1.call-done = (f32[3,384,768]{2,1,0:T(8,128)}, f32[384,768]{1,0:T(8,128)}) async-done(((f32[3,384,768]{2,1,0:T(8,128)}, f32[384,768]{1,0:T(8,128)}), (f32[3,384,768]{2,1,0:T(8,128)}, f32[384,768]{1,0:T(8,128)})) %all-reduce.13.cloned.1.call-update) | async-done | bytes 4718608 | tf_op jit(solution)/shard_map/psum | solution.py:247
  1392.4 4.1 copy.98
  1396.5 1.0 copy.99
  1397.5 1.1 copy-done.17
  1398.6 1.4 copy.100
  1400.0 1.1 copy-done.16
  1401.1 1.4 copy.101
  (156 shorter events, 14.4 us)
Async XLA Ops:
  7.2 74.8 %copy-start = (bf16[384,1536]{1,0:T(8,128)(2,1)S(1)}, bf16[384,1536]{1,0:T(8,128)(2,1)}, u32[]{:S(2)}) copy-start(bf16[384,1536]{1,0:T(8,128)(2,1)} %param.32) | copy-start | bytes 3538948
  7.2 5.0 copy-start.2
  7.2 5.0 copy-start.24
  7.2 5.0 copy-start.25
  7.2 69.8 %all-reduce.9.cloned.1.call-start = ((), (), s32[]{:S(2)}) async-start(), calls=%async_computation.6 | async-start | bytes 1572864 | tf_op jit(solution)/shard_map/psum | solution.py:127
  9.8 2.5 copy-start.31
  28.1 4.4 copy-start.14
  31.7 2.1 copy-start.10
  31.8 2.1 copy-start.11
  31.8 0.7 copy-start.18
  33.8 93.1 %reduce-scatter.11.cloned.1.call-start = ((), (), s32[]{:S(2)}) async-start(), calls=%async_computation.10 | async-start | bytes 4718592 | tf_op jit(solution)/shard_map/reduce_scatter | solution.py:160
  39.9 0.7 copy-start.39
  39.9 0.8 copy-start.26
  39.9 37.1 %copy-start.37 = (f32[768]{0:T(1024)S(1)}, f32[768]{0:T(1024)}, u32[]{:S(2)}) copy-start(f32[768]{0:T(1024)} %param.27) | copy-start | bytes 9220
  39.9 136.2 %reduce-scatter.7.cloned.1.call-start = ((), (), s32[]{:S(2)}) async-start(), calls=%async_computation.7 | async-start | bytes 4718592 | tf_op jit(solution)/shard_map/reduce_scatter | solution.py:141
  81.2 0.8 copy-start.5
  84.6 91.5 %copy-start.35 = (f32[1536]{0:T(1024)S(1)}, f32[1536]{0:T(1024)}, u32[]{:S(2)}) copy-start(f32[1536]{0:T(1024)} %param.33) | copy-start | bytes 18436
  84.6 126.6 %all-gather.5.cloned.1.call-start = ((), (), s32[]{:S(2)}) async-start(), calls=%async_computation.11 | async-start | bytes 2359296 | tf_op jit(solution)/shard_map/all_gather | solution.py:167
  180.4 46.7 %reduce-scatter.13.cloned.1.call-start = ((), (), s32[]{:S(2)}) async-start(), calls=%async_computation.12 | async-start | bytes 1179648 | tf_op jit(solution)/shard_map/reduce_scatter | solution.py:171
  214.5 45.2 %all-gather.3.cloned.1.call-start = ((), (), s32[]{:S(2)}) async-start(), calls=%async_computation.8 | async-start | bytes 2359296 | tf_op jit(solution)/shard_map/all_gather | solution.py:151
  215.1 60.0 %reduce-scatter.15.cloned.1.call-start = ((), (), s32[]{:S(2)}) async-start(), calls=%async_computation.13 | async-start | bytes 1179648 | tf_op jit(solution)/shard_map/reduce_scatter | solution.py:215
  239.7 1.0 copy-start.12
  239.7 1.8 copy-start.15
  240.0 1.5 copy-start.33
  241.5 3.0 copy-start.7
  242.7 3.8 copy-start.22
  248.0 2.5 copy-start.23
  248.0 2.5 copy-start.36
  254.5 35.9 %reduce-scatter.17.cloned.1.call-start = ((), (), s32[]{:S(2)}) async-start(), calls=%async_computation.14 | async-start | bytes 1179648 | tf_op jit(solution)/shard_map/reduce_scatter | solution.py:218
  255.2 210.5 %reduce-scatter.9.cloned.1.call-start = ((), (), s32[]{:S(2)}) async-start(), calls=%async_computation.9 | async-start | bytes 1179648 | tf_op jit(solution)/shard_map/reduce_scatter | solution.py:153
  263.4 204.3 %all-reduce.11.cloned.1.call-start = ((), (), s32[]{:S(2)}) async-start(), calls=%async_computation.15 | async-start | bytes 1572864 | tf_op jit(solution)/shard_map/psum | solution.py:243
  293.1 3.8 copy-start.6
  293.1 522.4 %all-reduce.15.cloned.1.call-start = ((), (), s32[]{:S(2)}) async-start(), calls=%async_computation.17 | async-start | bytes 9437184 | tf_op jit(solution)/shard_map/psum | solution.py:43
  293.2 3.8 copy-start.4
  299.2 1.0 copy-start.8
  299.2 1.0 copy-start.19
  299.2 2.4 copy-start.9
  299.2 1093.2 %all-reduce.13.cloned.1.call-start = ((), (), s32[]{:S(2)}) async-start(), calls=%async_computation.16 | async-start | bytes 9437184 | tf_op jit(solution)/shard_map/psum | solution.py:247
  300.2 1.8 copy-start.20
  304.6 161.1 %copy-start.27 = (f32[6,64]{1,0:T(8,128)S(1)}, f32[6,64]{1,0:T(8,128)}, u32[]{:S(2)}) copy-start(f32[6,64]{1,0:T(8,128)} %get-tuple-element.372) | copy-start | bytes 4612
  304.6 161.2 %copy-start.38 = (f32[384]{0:T(512)S(1)}, f32[384]{0:T(512)}, u32[]{:S(2)}) copy-start(f32[384]{0:T(512)} %param.35) | copy-start | bytes 4612
  306.4 162.7 %copy-start.32 = (f32[256]{0:T(256)S(1)}, f32[256]{0:T(256)}, u32[]{:S(2)}) copy-start(f32[256]{0:T(256)} %copy-done.31) | copy-start | bytes 3076
  467.4 2.2 copy-start.28
  467.4 2.2 copy-start.29
  467.4 2.2 copy-start.30
  467.4 346.8 %copy-start.13 = (bf16[256,768]{1,0:T(8,128)(2,1)S(1)}, bf16[256,768]{1,0:T(8,128)(2,1)}, u32[]{:S(2)}) copy-start(bf16[256,768]{1,0:T(8,128)(2,1)} %param.23) | copy-start | bytes 1179652
  467.4 346.8 %copy-start.34 = (f32[256]{0:T(256)S(1)}, f32[256]{0:T(256)}, u32[]{:S(2)}) copy-start(f32[256]{0:T(256)} %copy-done.33) | copy-start | bytes 3076
  467.7 1.5 copy-start.3
  1392.4 4.1 copy-start.21
  1396.5 2.1 copy-start.17
  1398.6 2.5 copy-start.16
  1398.6 3.9 copy-start.1
Sparse Core Ops, SparseCore 0:
  33.9 43.0 all-reduce.8
  80.0 46.8 reduce-scatter.10
  129.3 46.8 reduce-scatter.6
  180.5 30.6 all-gather.4
  214.6 12.3 reduce-scatter.12
  229.1 30.5 all-gather.2
  262.7 12.3 reduce-scatter.14
  278.1 12.2 reduce-scatter.16
  293.3 12.2 reduce-scatter.8
  308.1 42.3 all-reduce.10
  353.6 366.1 all-reduce.14
  722.8 669.4 all-reduce.12
where the time goes:
time: 1410 us
  waiting for transfers between devices  774 us (55%)
  blocking collectives  525 us (37%)
  matrix products  46.7 us (3%)
  other arithmetic  26.3 us (2%)
  local copies, waits for them, and re-layouts  21.4 us (2%)
  between operations  14.7 us (1%)
    psum x1, waiting for transfers between devices, per_device(): lax.psum((grad_qkv_weight, grad_qv_bias, grad_out_weight, grad_out_bias,...  577 us
    psum x1, blocking collectives, per_device(): lax.psum((grad_qkv_weight, grad_qv_bias, grad_out_weight, grad_out_bias,...  345 us
    psum x1, blocking collectives, sum_mlp(): return lax.psum((grads[0], grads[1], grads[2], grads[3]), 'dp')  159 us
    reduce_scatter x1, waiting for transfers between devices, per_device(): lax.psum_scatter(jnp.dot(piece, up_weight, preferred_element_type=f32), '...  49.2 us
    reduce_scatter x1, waiting for transfers between devices, per_device(): lax.psum_scatter(jnp.dot(piece, down_weight, preferred_element_type=f32),...  42.2 us
    psum x1, waiting for transfers between devices, per_device(): lax.psum(jnp.dot(attended_low, out_weight, preferred_element_type=f32), '...  36.3 us
    all_gather x1, waiting for transfers between devices, per_device(): grad_pre_all = lax.all_gather(grad_pre, 'mp', axis=0, tiled=True)  30.8 us
  transfers between devices with their start and end apart: 12, of which 9 were waited for; matrix products, arithmetic and copies ran while one was open for 4% of the time, Pallas kernels for 0%

commit v1 on v0

v1 whole, which is shorter than its diff:
```python
import functools

import jax
import jax.numpy as jnp
from jax import lax
from jax.experimental import pallas as pl
from jax.experimental.pallas import tpu as pltpu
from jax.sharding import PartitionSpec as P

HD = 64
EPS = 1e-05
NEG = -1e30
MESH = pl.DeviceIdType.MESH
F32, BF16 = jnp.float32, jnp.bfloat16
def place():
    dp = lax.axis_index("dp")
    xh = lax.rem(dp, 2); y = lax.rem(lax.div(dp, 2), 4); z = lax.div(dp, 8)
    def at(z, y, xh):
        return {"dp": z * 8 + y * 2 + xh}
    y1 = y + 1 - 2 * lax.rem(y, 2)
    z1 = z + 1 - 2 * lax.rem(z, 2)
    peers = [at(z, y1, xh), at(z1, y, xh), at(z, 3 - y, xh), at(3 - z, y, xh), at(z, y, 1 - xh)]
    bits = [lax.rem(lax.div(y + 1, 2), 2), lax.rem(lax.div(z + 1, 2), 2), lax.div(y, 2), lax.div(z, 2), xh]
    return peers, bits

def ar_kernel(R, g_ref, out_ref, acc, sbuf, rbuf, ssem, rsem, asem, bsem):
    Q = R // 4
    peers, bits = place()
    bar = pltpu.get_barrier_semaphore()
    for p in peers:
        pl.semaphore_signal(bar, inc=1, device_id=p, device_id_type=MESH)
    pl.semaphore_wait(bar, 5)
    C = R // 64
    def rs_copy(s, k):
        L = Q >> (min(k, 3) + 1)
        o = s * Q + (Q - (Q >> k))
        d = (s + k) % 4 if k < 4 else 4
        return pltpu.make_async_remote_copy(
            src_ref=sbuf.at[pl.ds(o, L)], dst_ref=rbuf.at[pl.ds(o, L)],
            send_sem=ssem.at[s, k], recv_sem=rsem.at[s, k], device_id=peers[d], device_id_type=MESH)
    offs = [jnp.int32(s * Q) for s in range(4)]
    m8 = lambda v: pl.multiple_of(v, 16)
    hist = []
    for k in range(4):
        L = Q >> (k + 1)
        keep, give = [], []
        for s in range(4):
            b = bits[(s + k) % 4]
            keep.append(offs[s] + b * L); give.append(offs[s] + (1 - b) * L)
        for s in range(4):
            if k > 0:
                rs_copy(s, k - 1).wait_recv()
            so = s * Q + (Q - (Q >> k))
            po = s * Q + (Q - (Q >> (k - 1))) if k > 0 else 0
            go = give[s]
            rel = go - offs[s]
            @pl.loop(0, L // C)
            def _(i):
                v = (g_ref if k < 2 else acc)[pl.ds(m8(go + i * C), C), :]
                if k > 0:
                    v = v + rbuf[pl.ds(m8(po + rel + i * C), C), :].astype(F32)
                sbuf[pl.ds(m8(so + i * C), C), :] = v.astype(BF16)
            rs_copy(s, k).start()
        if k > 0:
            for s in range(4):
                ko = keep[s]
                rel = ko - offs[s]
                po = s * Q + (Q - (Q >> (k - 1)))
                @pl.loop(0, L // C)
                def _(i):
                    acc[pl.ds(m8(ko + i * C), C), :] = (g_ref if k == 1 else acc)[pl.ds(m8(ko + i * C), C), :] + rbuf[pl.ds(m8(po + rel + i * C), C), :].astype(F32)
        hist.append(list(offs))
        offs = keep
    xh = bits[4]
    L = Q // 16
    for s in range(4):
        rs_copy(s, 3).wait_recv()
    for j in range(2):
        for s in (2 * j, 2 * j + 1):
            po = s * Q + (Q - (Q >> 3))
            so = s * Q + (Q - (Q >> 4))
            sbuf[pl.ds(so, L), :] = (acc[pl.ds(m8(offs[s]), L), :] + rbuf[pl.ds(po, L), :].astype(F32)).astype(BF16)
    def x_copy(j):
        o = (2 * j + (1 - xh)) * Q + Q - (Q >> 4)
        return pltpu.make_async_remote_copy(
            src_ref=sbuf.at[pl.ds(m8(o), L)], dst_ref=rbuf.at[pl.ds(m8(o), L)],
            send_sem=ssem.at[j, 4], recv_sem=rsem.at[j, 4], device_id=peers[4], device_id_type=MESH)
    for j in range(2):
        x_copy(j).start()
    for j in range(2):
        x_copy(j).wait_recv()
    def fin_off(j, h):
        return jnp.where(h == 0, offs[2 * j], offs[2 * j + 1]) if False else offs[2 * j] + h * (offs[2 * j + 1] - offs[2 * j])
    def ax_copy(j):
        o = fin_off(j, xh)
        return pltpu.make_async_remote_copy(
            src_ref=out_ref.at[pl.ds(m8(o), L)], dst_ref=out_ref.at[pl.ds(m8(o), L)],
            send_sem=asem.at[j, 4], recv_sem=bsem.at[j, 4], device_id=peers[4], device_id_type=MESH)
    for j in range(2):
        s = 2 * j + xh
        po = m8(s * Q + (Q - (Q >> 3)))
        ro = m8(s * Q + (Q - (Q >> 4)))
        fo = m8(fin_off(j, xh))
        out_ref[pl.ds(fo, L), :] = (acc[pl.ds(fo, L), :] + rbuf[pl.ds(po, L), :].astype(F32) + rbuf[pl.ds(ro, L), :].astype(F32)).astype(BF16)
        ax_copy(j).start()
    for j in range(2):
        ax_copy(j).wait_recv()
    def ag_copy(s, k):
        L = Q >> (k + 1)
        d = (s + k) % 4
        o = m8(hist[k][s] + bits[d] * L)
        return pltpu.make_async_remote_copy(
            src_ref=out_ref.at[pl.ds(o, L)], dst_ref=out_ref.at[pl.ds(o, L)],
            send_sem=asem.at[s, k], recv_sem=bsem.at[s, k], device_id=peers[d], device_id_type=MESH)
    for k in (3, 2, 1, 0):
        for s in range(4):
            if k < 3:
                ag_copy(s, k + 1).wait_recv()
            ag_copy(s, k).start()
    for s in range(4):
        ag_copy(s, 0).wait_recv()
    for s in range(4):
        for k in range(4):
            rs_copy(s, k).wait_send()
            ag_copy(s, k).wait_send()
    for j in range(2):
        x_copy(j).wait_send()
        ax_copy(j).wait_send()

def all_reduce(g, cid):
    R = g.shape[0]
    return pl.pallas_call(
        functools.partial(ar_kernel, R),
        out_shape=jax.ShapeDtypeStruct((R, 128), BF16),
        in_specs=[pl.BlockSpec(memory_space=pltpu.VMEM)],
        out_specs=pl.BlockSpec(memory_space=pltpu.VMEM),
        scratch_shapes=[pltpu.VMEM((R, 128), F32), pltpu.VMEM((R, 128), BF16), pltpu.VMEM((R, 128), BF16)] + [pltpu.SemaphoreType.DMA((4, 5))] * 4,
        compiler_params=pltpu.CompilerParams(collective_id=cid, has_side_effects=True, vmem_limit_bytes=40 << 20),
        name="ar",
    )(g)


def dot(left, right, left_dim, right_dim):
    return lax.dot_general(
        left, right, (((left_dim,), (right_dim,)), ((), ())), preferred_element_type=F32
    )


def norm_stats(values):
    mean_row = jnp.mean(values, axis=-1, keepdims=True)
    centred = values - mean_row
    spread = jnp.mean(centred * centred, axis=-1, keepdims=True)
    scale = lax.rsqrt(spread + EPS)
    return centred * scale, scale


def gelu_parts(pre):
    c = 0.7978845608028654
    inner = c * (pre + 0.044715 * pre * pre * pre)
    t = jnp.tanh(inner)
    hidden = 0.5 * pre * (1.0 + t)
    slope = 0.5 * (1.0 + t) + 0.5 * pre * (1.0 - t * t) * (c * (1.0 + 3 * 0.044715 * pre * pre))
    return hidden, slope


def stage_attend(x, length, qkv, qv_bias, gain, shift):
    n1, _ = norm_stats(x.astype(F32))
    normed1 = (n1 * gain + shift).astype(BF16)
    q = (dot(normed1, qkv[0], 1, 1) + qv_bias[0]).astype(BF16)
    k = dot(normed1, qkv[1], 1, 1).astype(BF16)
    v = (dot(normed1, qkv[2], 1, 1) + qv_bias[1]).astype(BF16)
    probs_all, att = [], []
    rows = x.shape[0]
    qp = lax.broadcasted_iota(jnp.int32, (rows, rows), 0)
    kp = lax.broadcasted_iota(jnp.int32, (rows, rows), 1)
    allowed = (kp == qp) | ((kp < qp) & (qp < length))
    for h in range(q.shape[1] // HD):
        sl = slice(h * HD, (h + 1) * HD)
        s = jnp.where(allowed, dot(q[:, sl], k[:, sl], 1, 1) * HD**-0.5, NEG)
        e = jnp.where(allowed, jnp.exp(s - jnp.max(s, axis=-1, keepdims=True)), 0.0)
        p = e / jnp.sum(e, axis=-1, keepdims=True)
        probs_all.append(p)
        att.append(dot(p.astype(BF16), v[:, sl], 1, 0))
    return normed1, q, k, v, probs_all, jnp.concatenate(att, axis=1).astype(BF16)


def per_device(tokens, seq_lengths, cotangent, qkv_weight, qv_bias, out_weight, out_bias,
               first_gain, first_shift, second_gain, second_shift, up_weight, up_bias, down_weight, down_bias):
    j, i = lax.axis_index("grid"), lax.axis_index("mp")
    rpd = tokens.shape[0]
    own = qkv_weight.shape[1] // 2
    part = out_weight.shape[0]
    up_all = lax.all_gather(up_weight, "mp", axis=0, tiled=True)
    down_all = lax.all_gather(down_weight, "mp", axis=0, tiled=True)
    out_all = lax.all_gather(out_weight, "mp", axis=0, tiled=True)
    x = lax.all_gather(tokens, "grid", axis=0, tiled=True)
    cot = lax.all_gather(cotangent, "grid", axis=0, tiled=True)
    qkv = lax.dynamic_slice_in_dim(qkv_weight, own * j, own, 1)
    qvb = lax.dynamic_slice_in_dim(qv_bias, own * j, own, 1)
    out_own = lax.dynamic_slice_in_dim(out_weight, own * j, own, 0)
    normed1, q, k, v, probs, att = stage_attend(x, seq_lengths[0], qkv, qvb, first_gain, first_shift)
    att_all = lax.all_gather(att, ("mp", "grid"), axis=1, tiled=True)
    hidden1 = x.astype(F32) + dot(att_all, out_all, 1, 0) + out_bias
    n2, scale2 = norm_stats(hidden1)
    normed2 = (n2 * second_gain + second_shift).astype(BF16)
    pre = dot(normed2, up_all, 1, 0) + up_bias
    hidden, slope = gelu_parts(pre)
    hidden = hidden.astype(BF16)
    cot_part = lax.dynamic_slice_in_dim(cot, part * i, part, 1)
    n2_part = lax.dynamic_slice_in_dim(normed2, part * i, part, 1)
    mlp = lax.psum_scatter(dot(hidden, down_weight, 1, 1), "grid", scatter_dimension=0, tiled=True)
    h1_part = lax.dynamic_slice(hidden1, (rpd * j, part * i), (rpd, part))
    layer_out = (h1_part + mlp + down_bias).astype(BF16)
    grad_down = dot(cot_part, hidden, 0, 0)
    grad_down_bias = jnp.sum(cot_part.astype(F32), axis=0)
    grad_pre = (dot(cot, down_all, 1, 0) * slope).astype(BF16)
    grad_up = dot(n2_part, grad_pre, 0, 0)
    grad_up_bias = jnp.sum(grad_pre.astype(F32), axis=0)
    gn2 = lax.psum(dot(grad_pre, up_all, 1, 1), "grid")
    cotf = cot.astype(F32)
    e2 = gn2 * second_gain
    gh1 = cotf + (e2 - jnp.mean(e2, -1, keepdims=True) - n2 * jnp.mean(e2 * n2, -1, keepdims=True)) * scale2
    g2gain = jnp.sum(gn2 * n2, axis=0)
    g2shift = jnp.sum(gn2, axis=0)
    gb = gh1.astype(BF16)
    grad_out = dot(att, gb, 0, 0)
    grad_out_bias = jnp.sum(gb.astype(F32), axis=0)
    gatt = dot(gb, out_own, 1, 1).astype(BF16)
    gq, gk, gv = [], [], []
    for h in range(own // HD):
        sl = slice(h * HD, (h + 1) * HD)
        gp = dot(gatt[:, sl], v[:, sl], 1, 1)
        delta = jnp.sum(probs[h] * gp, axis=-1, keepdims=True)
        gs = (probs[h] * (gp - delta)).astype(BF16)
        gq.append(dot(gs, k[:, sl], 1, 0) * HD**-0.5)
        gk.append(dot(gs, q[:, sl], 0, 0) * HD**-0.5)
        gv.append(dot(probs[h].astype(BF16), gatt[:, sl], 0, 0))
    g3 = [jnp.concatenate(g, axis=1).astype(BF16) for g in (gq, gk, gv)]
    grad_qkv = jnp.concatenate([dot(g, normed1, 0, 0) for g in g3], axis=0)
    gqvb = jnp.stack([jnp.sum(g3[0].astype(F32), 0), jnp.sum(g3[2].astype(F32), 0)])
    gn1 = dot(g3[0], qkv[0], 1, 0) + dot(g3[1], qkv[1], 1, 0) + dot(g3[2], qkv[2], 1, 0)
    n1, scale1 = norm_stats(x.astype(F32))
    g1 = lax.psum(jnp.stack([jnp.sum(gn1 * n1, 0), jnp.sum(gn1, 0)]), ("mp", "grid"))
    gn1_mine = lax.psum(lax.psum_scatter(gn1, "grid", scatter_dimension=0, tiled=True), "mp")
    mine = lambda a: lax.dynamic_slice_in_dim(a, rpd * j, rpd, 0)
    e1 = gn1_mine * first_gain
    n1m = mine(n1)
    input_grad = mine(gh1) + (
        e1 - jnp.mean(e1, -1, keepdims=True) - n1m * jnp.mean(e1 * n1m, -1, keepdims=True)
    ) * mine(scale1)
    mlp_flat = jnp.concatenate([grad_up.reshape(-1, 128), grad_down.reshape(-1, 128)])
    smalls = [gqvb, grad_out_bias, g1, g2gain, g2shift, grad_up_bias, grad_down_bias]
    flat = jnp.concatenate([a.reshape(-1) for a in smalls])
    attn_flat = jnp.concatenate([grad_qkv.reshape(-1, 128), grad_out.reshape(-1, 128)])
    rows = 1024 - attn_flat.shape[0] % 1024
    attn_flat = jnp.concatenate([attn_flat, jnp.pad(flat, (0, rows * 128 - flat.shape[0])).reshape(rows, 128)])
    red = all_reduce(jnp.concatenate([mlp_flat, attn_flat]), 0).astype(F32)
    n_mlp = mlp_flat.shape[0]
    r_up = red[: n_mlp // 2].reshape(grad_up.shape)
    r_down = red[n_mlp // 2 : n_mlp].reshape(grad_down.shape)
    r_qkv = red[n_mlp : n_mlp + 3 * own * 6].reshape(3, own, 768)
    r_out = red[n_mlp + 18 * own : n_mlp + 24 * own].reshape(own, 768)
    sm = red[n_mlp + 24 * own :].reshape(-1)
    res, at = [], 0
    for a in smalls:
        res.append(sm[at : at + a.size].reshape(a.shape))
        at += a.size
    r_qkv = lax.all_gather(r_qkv.astype(BF16), "grid", axis=1, tiled=True).astype(F32)
    r_out = lax.all_gather(r_out.astype(BF16), "grid", axis=0, tiled=True).astype(F32)
    r_qvb = lax.all_gather(res[0], "grid", axis=1, tiled=True)
    return (layer_out, input_grad, r_qkv, r_qvb, r_out, res[1], res[2][0], res[2][1], res[3], res[4],
            r_up, res[5], r_down, res[6])


def solution(mesh):
    placed = (
        P(("dp", "grid"), None), P("dp"), P(("dp", "grid"), None), P(None, "mp", None), P(None, "mp"),
        P("mp", None), P(), P(), P(), P(), P(), P("mp", "grid"), P("grid"), P("mp", "grid"), P("mp"),
    )
    return jax.shard_map(
        per_device,
        mesh=mesh,
        in_specs=placed,
        out_specs=(
            P(("dp", "grid"), "mp"), P(("dp", "grid"), None), P(None, "mp", None), P(None, "mp"), P("mp", None),
            P(), P(), P(), P(), P(), P("mp", "grid"), P("grid"), P("mp", "grid"), P("mp"),
        ),
        check_vma=False,
    )
```

time: 1410 us -> 367 us (0.26)
  waiting for transfers between devices: 774 us -> 125 us
  blocking collectives: 525 us -> 37.4 us
  Pallas kernels: 0 us -> 58.7 us
  local copies, waits for them, and re-layouts: 21.4 us -> 52.1 us
    psum x4 -> x2, waiting for transfers between devices: 613 us -> 50.6 us  [the longest x1 27.3 us: per_device(): gn2 = lax.psum(dot(grad_pre, up_all, 1, 1), 'grid')]
    psum x2 -> x1, blocking collectives: 504 us -> 5.44 us  [per_device(): lax.psum(jnp.stack([jnp.sum(gn1 * n1, 0), jnp.sum(gn1, 0)]), ('mp', 'grid'))]
    reduce_scatter x6 -> x2, waiting for transfers between devices: 125 us -> 0.01 us  [the longest x1 0.01 us: per_device(): lax.psum_scatter(gn1, 'grid', scatter_dimension=0, tiled=True)]
    pallas_call x0 -> x1, Pallas kernels: none -> 58.7 us  [all_reduce(): pl.pallas_call(functools.partial(ar_kernel, R), out_shape=jax.ShapeDtypeS...]
    all_gather x2 -> x4, waiting for transfers between devices: 35.3 us -> 72.6 us  [the longest x1 36.3 us: per_device(): down_all = lax.all_gather(down_weight, 'mp', axis=0, tiled=True)]
    reshape x0 -> x9, local copies, waits for them, and re-layouts: none -> 15.6 us  [the longest x1 3.25 us: per_device(): r_up = red[:n_mlp // 2].reshape(grad_up.shape)]
    dot_general x25 -> x36, matrix products: 46.7 us -> 47.3 us  [dot(): lax.dot_general(left, right, (((left_dim,), (right_dim,)), ((), ())), pre...]
  transfers between devices with their start and end apart: 12 -> 8, of which waited for: 9 -> 4; matrix products, arithmetic and copies ran while one was open for 4% -> 24% of each run, Pallas kernels for 0% -> 16%
where the time goes in v1:
time: 367 us; the launch traced here: 365 us
  waiting for transfers between devices  125 us (34%)
  Pallas kernels  58.7 us (16%)
  local copies, waits for them, and re-layouts  52.1 us (14%)
  matrix products  47.3 us (13%)
  blocking collectives  37.4 us (10%)
  other arithmetic  28.4 us (8%)
  between operations  15.8 us (4%)
    pallas_call x1, Pallas kernels, all_reduce(): pl.pallas_call(functools.partial(ar_kernel, R), out_shape=jax.ShapeDtypeS...  58.7 us
    dot_general x36, matrix products, dot(): lax.dot_general(left, right, (((left_dim,), (right_dim,)), ((), ())), pre...  47.3 us
    all_gather x1, waiting for transfers between devices, per_device(): down_all = lax.all_gather(down_weight, 'mp', axis=0, tiled=True)  36.3 us
    all_gather x1, waiting for transfers between devices, per_device(): up_all = lax.all_gather(up_weight, 'mp', axis=0, tiled=True)  36.2 us
    psum x1, waiting for transfers between devices, per_device(): gn2 = lax.psum(dot(grad_pre, up_all, 1, 1), 'grid')  27.3 us
    unnamed x177, local copies, waits for them, and re-layouts  24.2 us
    psum x1, waiting for transfers between devices, per_device(): lax.psum(lax.psum_scatter(gn1, 'grid', scatter_dimension=0, tiled=True),...  23.3 us
    all_gather x1, blocking collectives, per_device(): att_all = lax.all_gather(att, ('mp', 'grid'), axis=1, tiled=True)  13.9 us
  transfers between devices with their start and end apart: 8, of which 4 were waited for; matrix products, arithmetic and copies ran while one was open for 24% of the time, Pallas kernels for 16%

profile of v1, /device:TPU:1, one launch (start us, length us, event | category | flops | bytes accessed | tf_op | source)
XLA Modules:
  0.0 365.5 jit_solution(5675075736003341487)
XLA Ops:
  8.0 0.7 all-gather.8.cloned.1.call-update
  10.2 3.4 all_gather.27
  16.1 1.3 fusion.97
  17.4 1.4 fusion.96
  18.8 1.4 fusion.95
  20.6 0.8 copy-done.14
  21.4 2.1 fusion.25
  24.1 0.8 copy-done.16
  26.3 2.5 all_gather.31
  28.8 13.9 %all_gather.28 = bf16[512,768]{0,1:T(8,128)(2,1)} all-gather(bf16[512,192]{0,1:T(8,128)(2,1)S(1)} %pad_maximum_fusion.1), channel_id=1, replica_groups=mesh['dp'=32,'mp'=2,'grid'=2] {'mp','grid'}, dimensions={1}, use_global_device_ids=true | all-gather | bytes 983040 | tf_op jit(solution)/shard_map/all_gather | solution.py:202
  42.8 2.7 fusion.98
  46.3 1.2 add_convert_fusion
  47.5 36.2 %all-gather.8.cloned.1.call-done = bf16[768,1536]{1,0:T(8,128)(2,1)} async-done(((bf16[384,1536]{1,0:T(8,128)(2,1)}), bf16[768,1536]{1,0:T(8,128)(2,1)}) %all-gather.8.cloned.1.call-update) | async-done | bytes 2359312 | tf_op jit(solution)/shard_map/all_gather | solution.py:193
  83.8 4.9 %convolution_add_fusion = f32[512,1536]{1,0:T(8,128)} fusion(bf16[512,768]{1,0:T(8,128)(2,1)} %add_convert_fusion, bf16[768,1536]{1,0:T(8,128)(2,1)} %all-gather.8.cloned.1.call-done, f32[1536]{0:T(1024)} %param.27), kind=kOutput, calls=%fused_computation.3 | convolution fusion | flops 1208745984 | bytes 6297600 | tf_op jit(solution)/shard_map/dot_general | solution.py:144
  88.7 36.3 %all-gather.10.cloned.1.call-done = bf16[768,1536]{1,0:T(8,128)(2,1)} async-done(((bf16[384,1536]{1,0:T(8,128)(2,1)}), bf16[768,1536]{1,0:T(8,128)(2,1)}) %all-gather.10.cloned.1.call-update) | async-done | bytes 2359312 | tf_op jit(solution)/shard_map/all_gather | solution.py:194
  125.0 6.4 %convert_reduce_fusion = (f32[1536]{0:T(1024)}, bf16[512,1536]{1,0:T(8,128)(2,1)S(1)}) fusion(f32[512,1536]{1,0:T(8,128)} %convolution_add_fusion, bf16[512,768]{1,0:T(8,128)(2,1)} %all_gather.31, bf16[768,1536]{1,0:T(8,128)(2,1)} %all-gather.10.cloned.1.call-done), kind=kOutput, calls=%fused_computation.10 | convolution fusion | flops 1224473088 | bytes 7870464 | tf_op jit(solution)/shard_map/dot_general | solution.py:144
  131.4 1.1 copy-done.23
  132.5 2.6 fusion.99
  135.3 27.3 %all-reduce.4.cloned.1.call-done = f32[512,768]{1,0:T(8,128)} async-done(((f32[512,768]{1,0:T(8,128)}), f32[512,768]{1,0:T(8,128)}) %all-reduce.4.cloned.1.call-update) | async-done | bytes 1572880 | tf_op jit(solution)/shard_map/psum | solution.py:219
  162.6 2.9 multiply_reduce_fusion
  165.5 1.9 convert_reduce_fusion.2
  167.9 1.3 copy-done.19
  169.6 0.9 copy-done.17
  170.9 0.9 copy-done.15
  172.8 0.8 multiply_reduce_fusion.7
  173.6 0.8 multiply_convert_fusion.3
  178.0 2.9 multiply_reduce_fusion.1
  181.0 1.0 copy-done.13
  182.1 4.7 %fusion.32 = f32[384,1536]{1,0:T(8,128)} fusion(bf16[512,768]{1,0:T(8,128)(2,1)S(1)} %copy-done.13, s32[]{:T(128)S(6)} %select_n.43, f32[512,1536]{1,0:T(8,128)} %convolution_add_fusion), kind=kOutput, calls=%fused_computation.90 | convolution fusion | flops 611057664 | bytes 5898244 | tf_op jit(solution)/shard_map/dot_general | solution.py:144
  186.8 3.2 reshape.149
  190.0 4.1 %fusion.30 = f32[384,1536]{1,0:T(8,128)} fusion(bf16[512,1536]{1,0:T(8,128)(2,1)} %copy-done.23, bf16[512,768]{1,0:T(8,128)(2,1)S(1)} %copy-done.22, s32[]{:T(128)S(6)} %select_n.43), kind=kOutput, calls=%fused_computation.87 | convolution fusion | flops 603979776 | bytes 4325380 | tf_op jit(solution)/shard_map/dot_general | solution.py:144
  194.1 3.2 reshape.148
  197.3 3.9 %fusion.87 = f32[512,384]{1,0:T(8,128)} fusion(bf16[384,1536]{1,0:T(8,128)(2,1)S(1)} %copy-done.25, f32[512,1536]{1,0:T(8,128)} %convolution_add_fusion), kind=kOutput, calls=%fused_computation.183 | convolution fusion | flops 611057664 | bytes 5111808 | tf_op jit(solution)/shard_map/dot_general | solution.py:144
  201.2 3.2 constant_dynamic-update-slice_fusion.4
  204.6 3.4 constant_dynamic-update-slice_fusion.3
  208.2 1.2 fusion.82
  209.9 1.1 fusion.43
  211.0 1.1 fusion.86
  212.3 2.6 pad_maximum_fusion
  214.9 0.9 reshape.151
  215.8 1.6 reshape.150
  217.4 5.4 %psum.23 = f32[1536]{0:T(1024)S(1)} all-reduce(f32[1536]{0:T(1024)S(1)} %reshape.153), channel_id=1, replica_groups=mesh['dp'=32,'mp'=2,'grid'=2] {'mp','grid'}, use_global_device_ids=true, to_apply=%region_26.27 | all-reduce | flops 1536 | bytes 12288 | tf_op jit(solution)/shard_map/psum | solution.py:243
  223.0 1.4 constant_dynamic-update-slice_fusion.2
  224.4 0.8 constant_dynamic-update-slice_fusion.1
  225.2 0.7 bitcast_dynamic-update-slice_fusion.g_ref
  226.0 3.1 copy-done.3
  229.0 58.7 %ar.1 = bf16[14336,128]{1,0:T(8,128)(2,1)S(1)} custom-call(f32[14336,128]{1,0:T(8,128)S(1)} %copy-done.3), custom_call_target="tpu_custom_call" | custom-call | tf_op jit(solution)/shard_map/ar/pallas_call | solution.py:132
  287.7 1.9 copy-done.2
  289.7 1.7 convert_element_type.120
  292.3 4.7 %convert_element_type.122 = f32[14336,128]{1,0:T(8,128)} convert(bf16[14336,128]{1,0:T(8,128)(2,1)} %copy-done.2) | non-fusion elementwise | flops 1835008 | bytes 11010048 | tf_op jit(solution)/shard_map/convert_element_type | solution.py:257
  297.0 9.9 %all-gather = f32[2,192,2]{1,2,0:T(2,128)S(1)} all-gather(f32[1,192,2]{1,2,0:T(2,128)S(1)} %bitcast.64), channel_id=1, replica_groups=mesh['dp'=32,'mp'=2,'grid'=2] {'grid'}, dimensions={0}, use_global_device_ids=true | all-gather | bytes 4608 | tf_op jit(solution)/shard_map/all_gather | solution.py:270
  307.9 1.3 slice_bitcast_fusion.6
  309.2 4.1 %fusion.94 = (f32[4608,128]{1,0:T(8,128)}, f32[4608,128]{1,0:T(8,128)}) fusion(bf16[14336,128]{1,0:T(8,128)(2,1)} %copy-done.2), kind=kLoop, calls=%fused_computation.184 | loop fusion | bytes 9437184 | tf_op jit(solution)/shard_map/slice | solution.py:260
  313.3 2.2 all_gather.35
  315.5 1.1 convert_element_type.124
  316.6 3.2 reshape.157
  319.9 3.2 reshape.156
  323.1 1.3 slice_bitcast_fusion
  324.4 1.4 slice_bitcast_fusion.1
  325.9 1.7 add_convert_fusion.2
  327.6 3.6 convert_element_type.121
  331.1 23.3 %all-reduce.6.cloned.1.call-done = f32[256,768]{1,0:T(8,128)} async-done(((f32[256,768]{1,0:T(8,128)}), f32[256,768]{1,0:T(8,128)}) %all-reduce.6.cloned.1.call-update) | async-done | bytes 786448 | tf_op jit(solution)/shard_map/psum | solution.py:244
  354.4 1.7 multiply_reduce_fusion.9
  356.2 2.5 multiply_add_fusion.2
  (237 shorter events, 15.9 us)
Async XLA Ops:
  7.2 8.0 %copy-start = (bf16[3,384,768]{2,1,0:T(8,128)(2,1)S(1)}, bf16[3,384,768]{2,1,0:T(8,128)(2,1)}, u32[]{:S(2)}) copy-start(bf16[3,384,768]{2,1,0:T(8,128)(2,1)} %param.18) | copy-start | bytes 5308420
  7.2 3.0 copy-start.40
  7.2 35.5 %all-gather.6.cloned.1.call-start = ((), (), s32[]{:S(2)}) async-start(), calls=%async_computation.2 | async-start | bytes 1769472 | tf_op jit(solution)/shard_map/all_gather | solution.py:195
  7.9 75.8 %all-gather.8.cloned.1.call-start = ((), (), s32[]{:S(2)}) async-start(), calls=%async_computation.3 | async-start | bytes 3538944 | tf_op jit(solution)/shard_map/all_gather | solution.py:193
  8.7 5.5 %copy-start.79 = (f32[2,384]{1,0:T(2,128)S(1)}, f32[2,384]{1,0:T(2,128)}, u32[]{:S(2)}) copy-start(f32[2,384]{1,0:T(2,128)} %param.19) | copy-start | bytes 9220
  8.7 6.1 %copy-start.50 = (f32[768]{0:T(1024)S(1)}, f32[768]{0:T(1024)}, u32[]{:S(2)}) copy-start(f32[768]{0:T(1024)} %param.22) | copy-start | bytes 9220
  8.7 6.1 %copy-start.73 = (f32[768]{0:T(1024)S(1)}, f32[768]{0:T(1024)}, u32[]{:S(2)}) copy-start(f32[768]{0:T(1024)} %param.23) | copy-start | bytes 9220
  8.7 116.3 %all-gather.10.cloned.1.call-start = ((), (), s32[]{:S(2)}) async-start(), calls=%async_computation.5 | async-start | bytes 3538944 | tf_op jit(solution)/shard_map/all_gather | solution.py:194
  9.5 153.2 %all-reduce.4.cloned.1.call-start = ((), (), s32[]{:S(2)}) async-start(), calls=%async_computation.6 | async-start | bytes 3145728 | tf_op jit(solution)/shard_map/psum | solution.py:219
  10.2 8.6 %copy-start.76 = (pred[512]{0:T(512)(128)(4,1)}, pred[512]{0:T(512)(128)(4,1)S(1)}, u32[]{:S(2)}) copy-start(pred[512]{0:T(512)(128)(4,1)S(1)} %iota_compare_fusion.2) | copy-start | bytes 1540
  13.6 2.0 copy-start.6
  14.2 1.9 copy-start.53
  15.2 5.0 %copy-start.4 = (bf16[512,768]{1,0:T(8,128)(2,1)}, bf16[512,768]{1,0:T(8,128)(2,1)S(1)}, u32[]{:S(2)}) copy-start(bf16[512,768]{1,0:T(8,128)(2,1)S(1)} %add_convert_fusion.1) | copy-start | bytes 2359300
  15.6 3.2 copy-start.26
  16.1 2.7 copy-start.48
  17.4 7.8 %copy-start.61 = (f32[512]{0:T(512)}, f32[512]{0:T(512)S(1)}, u32[]{:S(2)}) copy-start(f32[512]{0:T(512)S(1)} %get-tuple-element.47) | copy-start | bytes 6148
  17.4 2.8 copy-start.80
  18.8 5.3 %copy-start.63 = (f32[512]{0:T(512)}, f32[512]{0:T(512)S(1)}, u32[]{:S(2)}) copy-start(f32[512]{0:T(512)S(1)} %get-tuple-element.45) | copy-start | bytes 6148
  20.2 3.4 copy-start.65
  20.6 3.0 copy-start.18
  20.6 3.0 copy-start.77
  23.5 1.7 copy-start.71
  25.9 2.9 copy-start.46
  25.9 16.9 %copy-start.82 = (f32[768]{0:T(1024)S(1)}, f32[768]{0:T(1024)}, u32[]{:S(2)}) copy-start(f32[768]{0:T(1024)} %param.21) | copy-start | bytes 9220
  42.7 3.6 copy-start.51
  42.7 3.6 copy-start.74
  125.0 7.5 %copy-start.81 = (bf16[768,1536]{1,0:T(8,128)(2,1)S(1)}, bf16[768,1536]{1,0:T(8,128)(2,1)}, u32[]{:S(2)}) copy-start(bf16[768,1536]{1,0:T(8,128)(2,1)} %all-gather.8.cloned.1.call-done) | copy-start | bytes 7077892
  135.1 178.2 %reduce-scatter.5.cloned.1.call-start = ((), (), s32[]{:S(2)}) async-start(), calls=%async_computation.7 | async-start | bytes 2359296 | tf_op jit(solution)/shard_map/reduce_scatter | solution.py:244
  162.6 2.9 copy-start.11
  162.6 2.9 copy-start.12
  165.5 2.0 copy-start.24
  167.5 2.2 copy-start.8
  167.5 1.8 copy-start.19
  167.5 1.8 copy-start.66
  167.5 1.8 copy-start.68
  167.5 1.8 copy-start.78
  170.5 7.1 %copy-start.28 = (bf16[512,64]{0,1:T(8,128)(2,1)}, bf16[512,64]{0,1:T(8,128)(2,1)S(1)}, u32[]{:S(2)}) copy-start(bf16[512,64]{0,1:T(8,128)(2,1)S(1)} %convolution_convert_fusion.7) | copy-start | bytes 196612
  171.8 5.9 %copy-start.30 = (bf16[512,64]{0,1:T(8,128)(2,1)}, bf16[512,64]{0,1:T(8,128)(2,1)S(1)}, u32[]{:S(2)}) copy-start(bf16[512,64]{0,1:T(8,128)(2,1)S(1)} %convolution_convert_fusion.6) | copy-start | bytes 196612
  172.1 5.6 %copy-start.32 = (bf16[512,64]{0,1:T(8,128)(2,1)}, bf16[512,64]{0,1:T(8,128)(2,1)S(1)}, u32[]{:S(2)}) copy-start(bf16[512,64]{0,1:T(8,128)(2,1)S(1)} %convolution_convert_fusion.5) | copy-start | bytes 196612
  180.9 144.9 %reduce-scatter.3.cloned.1.call-start = ((), (), s32[]{:S(2)}) async-start(), calls=%async_computation.4 | async-start | bytes 1179648 | tf_op jit(solution)/shard_map/reduce_scatter | solution.py:211
  186.8 3.2 copy-start.22
  194.1 3.2 copy-start.25
  204.5 3.5 copy-start.29
  204.5 3.5 copy-start.31
  204.5 3.5 copy-start.33
  204.5 3.6 copy-start.43
  204.5 3.6 copy-start.45
  204.5 3.6 copy-start.47
  204.5 123.0 %all-gather.12.cloned.1.call-start = ((), (), s32[]{:S(2)}) async-start(), calls=%async_computation.9 | async-start | bytes 2654208 | tf_op jit(solution)/shard_map/all_gather | solution.py:268
  204.6 3.6 copy-start.9
  209.7 2.5 copy-start.56
  212.3 2.7 copy-start.55
  212.3 2.6 copy-start.21
  215.8 7.1 %copy-start.59 = (f32[768]{0:T(1024)S(1)}, f32[768]{0:T(1024)}, u32[]{:S(2)}) copy-start(f32[768]{0:T(1024)} %get-tuple-element.28) | copy-start | bytes 9220
  215.8 7.1 %copy-start.58 = (f32[768]{0:T(1024)S(1)}, f32[768]{0:T(1024)}, u32[]{:S(2)}) copy-start(f32[768]{0:T(1024)} %get-tuple-element.14) | copy-start | bytes 9220
  215.8 7.2 %copy-start.57 = (f32[768]{0:T(1024)S(1)}, f32[768]{0:T(1024)}, u32[]{:S(2)}) copy-start(f32[768]{0:T(1024)} %get-tuple-element.17) | copy-start | bytes 9220
  215.8 7.2 %copy-start.60 = (f32[1536]{0:T(1024)S(1)}, f32[1536]{0:T(1024)}, u32[]{:S(2)}) copy-start(f32[1536]{0:T(1024)} %get-tuple-element.53) | copy-start | bytes 18436
  225.9 3.1 copy-start.3
  287.7 1.9 copy-start.2
  291.5 63.0 %all-reduce.6.cloned.1.call-start = ((), (), s32[]{:S(2)}) async-start(), calls=%async_computation.8 | async-start | bytes 1572864 | tf_op jit(solution)/shard_map/psum | solution.py:244
  292.3 15.4 %slice-start = ((bf16[14336,128]{1,0:T(8,128)(2,1)}), bf16[1152,128]{1,0:T(8,128)(2,1)S(1)}, s32[]{:S(2)}) async-start(bf16[14336,128]{1,0:T(8,128)(2,1)} %copy-done.2), calls=%async_computation.10 | async-start | bytes 589824 | tf_op jit(solution)/shard_map/slice | solution.py:262
  319.9 6.0 %copy-start.75 = (f32[384]{0:T(512)S(1)}, f32[384]{0:T(512)}, u32[]{:S(2)}) copy-start(f32[384]{0:T(512)} %param.29) | copy-start | bytes 4612
  331.1 25.0 %copy-start.10 = (f32[512,768]{1,0:T(8,128)S(1)}, f32[512,768]{1,0:T(8,128)}, u32[]{:S(2)}) copy-start(f32[512,768]{1,0:T(8,128)} %copy-done.8) | copy-start | bytes 4718596
  354.4 4.2 %copy-start.1 = (bf16[3,384,768]{2,1,0:T(8,128)(2,1)S(1)}, bf16[3,384,768]{2,1,0:T(8,128)(2,1)}, u32[]{:S(2)}) copy-start(bf16[3,384,768]{2,1,0:T(8,128)(2,1)} %param.18) | copy-start | bytes 5308420
  (28 other events, 31.5 us)
Sparse Core Ops, SparseCore 0:
  9.7 32.7 all-gather.5
  44.2 39.5 all-gather.7
  85.4 39.5 all-gather.9
  135.2 27.3 all-reduce.3
  181.0 13.0 reduce-scatter.4
  204.6 12.1 reduce-scatter.2
  291.6 18.3 all-gather.11
  313.4 40.9 all-reduce.5

commit v2 on v1

v2 whole, which is shorter than its diff:
```python
import functools

import jax
import jax.numpy as jnp
from jax import lax
from jax.experimental import pallas as pl
from jax.experimental.pallas import tpu as pltpu
from jax.sharding import PartitionSpec as P

HD = 64
EPS = 1e-05
NEG = -1e30
MESH = pl.DeviceIdType.MESH
F32, BF16 = jnp.float32, jnp.bfloat16


def dot(left, right, left_dim, right_dim):
    return lax.dot_general(
        left, right, (((left_dim,), (right_dim,)), ((), ())), preferred_element_type=F32
    )


def up16(value):
    return pl.multiple_of(value, 16)


def cols128(start, size):
    return pl.ds(pl.multiple_of(start, 128), size)


class Place:
    def __init__(self):
        dp = lax.axis_index("dp")
        self.i, self.j = lax.axis_index("mp"), lax.axis_index("grid")
        self.xh, self.y, self.z = lax.rem(dp, 2), lax.rem(lax.div(dp, 2), 4), lax.div(dp, 8)
        self.sib = {"grid": 1 - self.j}
        self.xa = {"mp": 1 - self.i}
        self.xb = {"dp": dp + 1 - 2 * self.xh, "mp": 1 - self.i}
        self.xc = {"mp": 1 - self.i, "grid": 1 - self.j}
        self.far = {"dp": dp + 1 - 2 * self.xh}
        self.ring = (
            [{"dp": dp + 2 * (lax.rem(self.y + d, 4) - self.y)} for d in (1, 2, 3)],
            [{"dp": dp + 8 * (lax.rem(self.z + d, 4) - self.z)} for d in (1, 2, 3)],
        )

    def all(self):
        return [self.sib, self.xa, self.xb, self.xc, self.far] + self.ring[0] + self.ring[1]


class Copies:
    def __init__(self, send, recv):
        self.send, self.recv, self.made = send, recv, {}

    def put(self, name, src, dst, device):
        at = len(self.made)
        copy = pltpu.make_async_remote_copy(
            src_ref=src, dst_ref=dst, send_sem=self.send.at[at], recv_sem=self.recv.at[at],
            device_id=device, device_id_type=MESH)
        copy.start()
        self.made[name] = copy

    def got(self, name):
        self.made[name].wait_recv()

    def finish(self):
        for copy in self.made.values():
            copy.wait_send()


class Reduce:
    def __init__(self, tag, net, at, src, out, r1, p1, r2, p2, rx):
        self.tag, self.net, self.at = tag, net, at
        self.src, self.out, self.r1, self.p1, self.r2, self.p2, self.rx = src, out, r1, p1, r2, p2, rx
        self.half = src.shape[0] // 2
        self.big, self.small = self.half // 4, self.half // 16
        self.pos = ((at.y, at.z), (at.z, at.y))
        self.rings = ((at.ring[0], at.ring[1]), (at.ring[1], at.ring[0]))

    def start(self, s):
        for d in (1, 2, 3):
            to = lax.rem(self.pos[s][0] + d, 4)
            self.net.put((self.tag, 1, s, d), self.src.at[pl.ds(up16(s * self.half + to * self.big), self.big)],
                         self.r1.at[s, d - 1], self.rings[s][0][d - 1])

    def second(self, s):
        base = s * self.half + self.pos[s][0] * self.big
        for d in (1, 2, 3):
            self.net.got((self.tag, 1, s, d))
        for d in (1, 2, 3, 0):
            off = lax.rem(self.pos[s][1] + d, 4) * self.small
            rows = pl.ds(up16(off), self.small)
            total = self.src[pl.ds(up16(base + off), self.small), :].astype(F32)
            for e in range(3):
                total = total + self.r1[s, e, rows, :].astype(F32)
            self.p1[s, rows, :] = total.astype(BF16)
            if d:
                self.net.put((self.tag, 2, s, d), self.p1.at[s, rows], self.r2.at[s, d - 1], self.rings[s][1][d - 1])

    def third(self):
        for s in (0, 1):
            rows = pl.ds(up16(self.pos[s][1] * self.small), self.small)
            for d in (1, 2, 3):
                self.net.got((self.tag, 2, s, d))
            total = self.p1[s, rows, :].astype(F32)
            for e in range(3):
                total = total + self.r2[s, e].astype(F32)
            self.p2[s] = total.astype(BF16)
        self.net.put((self.tag, 3), self.p2.at[1 - self.at.xh], self.rx, self.at.far)

    def place(self, s):
        return s * self.half + self.pos[s][0] * self.big + self.pos[s][1] * self.small

    def own(self):
        self.net.got((self.tag, 3))
        where = up16(self.place(0) + self.at.xh * (self.place(1) - self.place(0)))
        rows = pl.ds(where, self.small)
        self.out[rows, :] = (self.p2[self.at.xh].astype(F32) + self.rx[...].astype(F32)).astype(BF16)
        self.net.put((self.tag, 4), self.out.at[rows], self.out.at[rows], self.at.far)

    def back(self):
        self.net.got((self.tag, 4))
        for s in (0, 1):
            rows = pl.ds(up16(self.place(s)), self.small)
            for d in (1, 2, 3):
                self.net.put((self.tag, 5, s, d), self.out.at[rows], self.out.at[rows], self.rings[s][1][d - 1])

    def spread(self):
        for s in (0, 1):
            rows = pl.ds(up16(s * self.half + self.pos[s][0] * self.big), self.big)
            for d in (1, 2, 3):
                self.net.got((self.tag, 5, s, d))
            for d in (1, 2, 3):
                self.net.put((self.tag, 6, s, d), self.out.at[rows], self.out.at[rows], self.rings[s][0][d - 1])

    def end(self):
        for s in (0, 1):
            for d in (1, 2, 3):
                self.net.got((self.tag, 6, s, d))


def column_sum8(values):
    return jnp.sum(values.reshape(values.shape[0] // 8, 8, values.shape[1]), axis=0)


S_QB, S_VB, S_OB, S_G1, S_H1, S_G2, S_H2, S_UB, S_DB, S_ROWS = 0, 2, 4, 10, 16, 22, 28, 34, 46, 64
V_OB, V_G1, V_H1, V_G2, V_H2, V_UB, V_DB = range(7)


def layer_kernel(
    length_ref, tokens, cotangent, qkv_ref, out_ref, up_ref, down_ref, vec, vec_up, qvb,
    lo_ref, ig_ref, om_ref, oa_ref, ob_ref,
    x_all, cot, normed1, n1, scale1, wown, qkvt, attt, probs, out_all, up_oth, down_oth,
    h1, n2, scale2, normed2, n2t, cott, hid, gpre, gn, gn_sib, mo, mo_sib, gh1, gb, acc, small, gattt, gt,
    g1_own, g1_sib, g1_sum, g1_far, gn1_keep, gn1_out, gn1_in, gn1_mine, gn1_far,
    gm, ga, m1, mp1, m2, mp2, mx, a1, ap1, a2, ap2, ax, send, recv,
):
    at = Place()
    i, j = at.i, at.j
    bar = pltpu.get_barrier_semaphore()
    peers = at.all()
    for peer in peers:
        pl.semaphore_signal(bar, inc=1, device_id=peer, device_id_type=MESH)
    pl.semaphore_wait(bar, len(peers))
    net = Copies(send, recv)
    mine, theirs = pl.ds(up16(256 * j), 256), pl.ds(up16(256 * (1 - j)), 256)
    ipart, opart = cols128(384 * i, 384), cols128(384 * (1 - i), 384)
    ihalf = pl.ds(up16(384 * i), 384)

    net.put("tok", tokens, x_all.at[mine], at.sib)
    net.put("cot", cotangent, cot.at[mine], at.sib)
    for n, peer in enumerate((at.xa, at.xb)):
        part = pl.ds(192 * n, 192)
        net.put(("out", n), out_ref.at[part], out_all.at[pl.ds(up16(384 * i + 192 * n), 192)], peer)
    for name, src, dst in (("up", up_ref, up_oth), ("down", down_ref, down_oth)):
        for n, peer in enumerate((at.xa, at.xb)):
            part = pl.ds(192 * n, 192)
            net.put((name, n), src.at[part], dst.at[part], peer)

    x_all[mine, :] = tokens[...]
    cot[mine, :] = cotangent[...]
    out_all[ihalf, :] = out_ref[...]
    for t in range(3):
        wown[pl.ds(192 * t, 192), :] = qkv_ref[t, pl.ds(up16(192 * j), 192), :]

    def first_norm(start):
        @pl.loop(0, 4)
        def _(b):
            rows = pl.ds(up16(start + 64 * b), 64)
            v = x_all[rows, :].astype(F32)
            c = v - jnp.mean(v, axis=-1, keepdims=True)
            sc = lax.rsqrt(jnp.mean(c * c, axis=-1, keepdims=True) + EPS)
            n = c * sc
            n1[rows, :] = n
            scale1[rows, :] = jnp.broadcast_to(sc, (64, 128))
            normed1[rows, :] = (n * vec[V_G1 : V_G1 + 1, :] + vec[V_H1 : V_H1 + 1, :]).astype(BF16)

    first_norm(256 * j)
    net.got("tok")
    first_norm(256 * (1 - j))

    for t in range(3):
        r = dot(wown[192 * t : 192 * t + 192, :], normed1[...], 1, 1)
        if t == 0:
            r = (r + qvb[0:192, :]).astype(BF16).astype(F32) * (HD**-0.5)
        if t == 2:
            r = r + qvb[192:384, :]
        qkvt[192 * t : 192 * t + 192, :] = r.astype(BF16)

    length = length_ref[0]
    own_rows = 384 * i + 192 * j
    for h in range(3):
        for qb in range(2):
            kr = 256 * (qb + 1)
            qc = slice(256 * qb, 256 * qb + 256)
            kt = qkvt[192 + 64 * h : 256 + 64 * h, 0:kr]
            s = dot(kt, qkvt[64 * h : 64 * h + 64, qc], 0, 0)
            kp = lax.broadcasted_iota(jnp.int32, (kr, 256), 0)
            qp = lax.broadcasted_iota(jnp.int32, (kr, 256), 1) + 256 * qb
            s = jnp.where((kp == qp) | ((kp < qp) & (qp < length)), s, NEG)
            e = jnp.exp(s - jnp.max(s, axis=0, keepdims=True))
            p = e * (1.0 / jnp.sum(e, axis=0, keepdims=True))
            probs[h, 0:kr, qc] = p
            o = dot(qkvt[384 + 64 * h : 448 + 64 * h, 0:kr], p.astype(BF16), 1, 0)
            attt[pl.ds(up16(own_rows + 64 * h), 64), qc] = o.astype(BF16)
        rows = pl.ds(up16(own_rows + 64 * h), 64)
        for n, peer in enumerate((at.xc, at.xa, at.sib)):
            net.put(("att", h, n), attt.at[rows], attt.at[rows], peer)

    net.got("cot")
    cott[...] = cot[:, ipart].T
    small[...] = jnp.zeros_like(small)

    def put_small(row, value):
        for c in range(value.shape[1] // 128):
            small[row + c : row + c + 1, :] = value[:, 128 * c : 128 * c + 128]

    put_small(S_DB, jnp.sum(cot[:, ipart].astype(F32), axis=0, keepdims=True))
    for n in range(2):
        net.got(("out", n))
    for h in range(3):
        for n in range(3):
            net.got(("att", h, n))

    @pl.loop(0, 4)
    def _(b):
        rows = pl.ds(up16(128 * b), 128)
        v = x_all[rows, :].astype(F32) + dot(attt[:, cols128(128 * b, 128)], out_all[...], 0, 0)
        v = v + vec[V_OB : V_OB + 1, :]
        h1[rows, :] = v
        c = v - jnp.mean(v, axis=-1, keepdims=True)
        sc = lax.rsqrt(jnp.mean(c * c, axis=-1, keepdims=True) + EPS)
        n = c * sc
        n2[rows, :] = n
        scale2[rows, :] = jnp.broadcast_to(sc, (128, 128))
        normed2[rows, :] = (n * vec[V_G2 : V_G2 + 1, :] + vec[V_H2 : V_H2 + 1, :]).astype(BF16)

    n2t[...] = normed2[:, ipart].T
    for name in ("up", "down"):
        for n in range(2):
            net.got((name, n))

    @pl.loop(0, 6)
    def _(c):
        cs = cols128(256 * c, 256)
        pre = dot(normed2[:, ipart], up_ref[:, cs], 1, 0) + dot(normed2[:, opart], up_oth[:, cs], 1, 0)
        pre = pre + vec_up[:, cs]
        g = dot(cot[:, ipart], down_ref[:, cs], 1, 0) + dot(cot[:, opart], down_oth[:, cs], 1, 0)
        k = 0.7978845608028654
        sq = pre * pre
        t = jnp.tanh(pre * (k + (k * 0.044715) * sq))
        half = 0.5 + 0.5 * t
        hid[:, cs] = (pre * half).astype(BF16)
        slope = half + (pre * half) * (1.0 - t) * (k + (3 * 0.044715 * k) * sq)
        gp = (g * slope).astype(BF16)
        gpre[:, cs] = gp
        ub = jnp.sum(gp.astype(F32), axis=0, keepdims=True)
        acc[24:25, cs] = ub

    for c in range(2):
        rows = pl.ds(256 * c, 256)
        gn[rows, ipart] = dot(gpre[rows, :], up_ref[...], 1, 1).astype(BF16)
        gn[rows, opart] = dot(gpre[rows, :], up_oth[...], 1, 1).astype(BF16)
        net.put(("gn", c), gn.at[rows], gn_sib.at[rows], at.sib)

    big = Reduce("m", net, at, gm, om_ref, m1, mp1, m2, mp2, mx)
    for s, left, right in ((1, cott, hid), (0, n2t, gpre)):
        @pl.loop(0, 6)
        def _(c):
            r = dot(left[...], right[:, cols128(256 * c, 256)], 1, 0).astype(BF16)
            for b in range(2):
                gm[pl.ds(up16(4608 * s + 384 * (2 * c + b)), 384), :] = r[:, 128 * b : 128 * b + 128]
        big.start(s)

    mo[...] = dot(hid[theirs, :], down_ref[...], 1, 1)
    net.put("mo", mo, mo_sib, at.sib)
    lo_part = dot(hid[mine, :], down_ref[...], 1, 1) + h1[mine, ipart] + vec[V_DB : V_DB + 1, 0:384]

    acc[0:24, 0:768] = jnp.zeros((24, 768), F32)
    for c in range(2):
        net.got(("gn", c))

    @pl.loop(0, 8)
    def _(b):
        rows = pl.ds(up16(64 * b), 64)
        g = gn[rows, :].astype(F32) + gn_sib[rows, :].astype(F32)
        n = n2[rows, :]
        e = g * vec[V_G2 : V_G2 + 1, :]
        m = jnp.mean(e, axis=-1, keepdims=True)
        mn = jnp.mean(e * n, axis=-1, keepdims=True)
        v = cot[rows, :].astype(F32) + (e - m - n * mn) * scale2[rows, 0:1]
        gh1[rows, :] = v
        low = v.astype(BF16)
        gb[rows, :] = low
        acc[0:8, 0:768] += column_sum8(g * n)
        acc[8:16, 0:768] += column_sum8(g)
        acc[16:24, 0:768] += column_sum8(low.astype(F32))

    put_small(S_G2, jnp.sum(acc[0:8, 0:768], axis=0, keepdims=True))
    put_small(S_H2, jnp.sum(acc[8:16, 0:768], axis=0, keepdims=True))
    put_small(S_OB, jnp.sum(acc[16:24, 0:768], axis=0, keepdims=True))
    put_small(S_UB, acc[24:25, :])

    gattt[...] = dot(out_ref[pl.ds(up16(192 * j), 192), :], gb[...], 1, 1).astype(BF16)
    net.got("mo")
    lo_ref[...] = (lo_part + mo_sib[...]).astype(BF16)

    for h in range(3):
        hs = slice(64 * h, 64 * h + 64)
        gk, gv = [], []
        for qb in range(2):
            kr = 256 * (qb + 1)
            qc = slice(256 * qb, 256 * qb + 256)
            p = probs[h, 0:kr, qc]
            gat = gattt[hs, qc]
            g = dot(qkvt[384 + 64 * h : 448 + 64 * h, 0:kr], gat, 0, 0)
            delta = jnp.sum(p * g, axis=0, keepdims=True)
            gs = (p * (g - delta)).astype(BF16)
            gt[hs, qc] = (dot(qkvt[192 + 64 * h : 256 + 64 * h, 0:kr], gs, 1, 0) * (HD**-0.5)).astype(BF16)
            gk.append(dot(qkvt[hs, qc], gs, 1, 1))
            gv.append(dot(gat, p.astype(BF16), 1, 1))
        for base, parts in ((192, gk), (384, gv)):
            rows = slice(base + 64 * h, base + 64 * h + 64)
            gt[rows, 0:256] = (parts[0] + parts[1][:, 0:256]).astype(BF16)
            gt[rows, 256:512] = parts[1][:, 256:512].astype(BF16)
        if h == 0:
            big.second(1)
            big.second(0)
        elif h == 1:
            big.third()
        else:
            big.own()

    @pl.loop(0, 2)
    def _(b):
        rows = pl.ds(up16(128 * b), 128)
        r = dot(gt[:, cols128(256 * (1 - j) + 128 * b, 128)], wown[...], 0, 0)
        gn1_out[rows, :] = r.astype(BF16)
        gn1_keep[pl.ds(up16(256 * (1 - j) + 128 * b), 128), :] = r

    net.put("gn1", gn1_out, gn1_in, at.sib)

    @pl.loop(0, 2)
    def _(b):
        r = dot(gt[:, cols128(256 * j + 128 * b, 128)], wown[...], 0, 0)
        gn1_keep[pl.ds(up16(256 * j + 128 * b), 128), :] = r

    acc[0:16, 0:768] = jnp.zeros((16, 768), F32)

    @pl.loop(0, 8)
    def _(b):
        rows = pl.ds(up16(64 * b), 64)
        g = gn1_keep[rows, :]
        acc[0:8, 0:768] += column_sum8(g * n1[rows, :])
        acc[8:16, 0:768] += column_sum8(g)

    for n in range(2):
        g1_own[8 * n : 8 * n + 8, :] = jnp.broadcast_to(
            jnp.sum(acc[8 * n : 8 * n + 8, 0:768], axis=0, keepdims=True), (8, 768))
    net.put("g1", g1_own, g1_sib, at.sib)
    big.back()

    ones = jnp.ones((16, 512), BF16)
    for base, row in ((0, S_QB), (384, S_VB)):
        r = dot(ones, gt[base : base + 192, :], 1, 1)
        small[row : row + 1, :] = r[0:1, 0:128]
        small[row + 1 : row + 2, 0:64] = r[0:1, 128:192]
    for n in range(3):
        r = dot(gt[192 * n : 192 * n + 192, :], normed1[...], 1, 0).astype(BF16)
        for c in range(6):
            ga[pl.ds(576 * c + 192 * n, 192), :] = r[:, 128 * c : 128 * c + 128]
    r = dot(attt[pl.ds(up16(own_rows), 192), :], gb[...], 1, 0).astype(BF16)
    for c in range(6):
        ga[pl.ds(3456 + 192 * c, 192), :] = r[:, 128 * c : 128 * c + 128]
    ga[pl.ds(4608 + S_ROWS, 512 - S_ROWS), :] = jnp.zeros((512 - S_ROWS, 128), BF16)
    tail = Reduce("a", net, at, ga, oa_ref, a1, ap1, a2, ap2, ax)
    tail.start(0)

    net.got("g1")
    g1_sum[...] = g1_own[...] + g1_sib[...]
    net.put("g1x", g1_sum, g1_far, at.xa)
    net.got("gn1")
    half_sum = gn1_keep[mine, :] + gn1_in[...].astype(F32)
    gn1_mine[...] = half_sum.astype(BF16)
    net.put("gn1x", gn1_mine, gn1_far, at.xa)
    net.got("g1x")
    g1_own_sum = g1_sum[...] + g1_far[...]
    put_small(S_G1, g1_own_sum[0:1, :])
    put_small(S_H1, g1_own_sum[8:9, :])
    ga[pl.ds(4608, S_ROWS), :] = small[...].astype(BF16)
    tail.start(1)
    big.spread()
    tail.second(0)
    tail.second(1)
    tail.third()
    net.got("gn1x")

    @pl.loop(0, 4)
    def _(b):
        rows = pl.ds(up16(64 * b), 64)
        full = pl.ds(up16(256 * j + 64 * b), 64)
        g = gn1_mine[rows, :].astype(F32) + gn1_far[rows, :].astype(F32)
        n = n1[full, :]
        e = g * vec[V_G1 : V_G1 + 1, :]
        m = jnp.mean(e, axis=-1, keepdims=True)
        mn = jnp.mean(e * n, axis=-1, keepdims=True)
        ig_ref[rows, :] = gh1[full, :] + (e - m - n * mn) * scale1[full, 0:1]

    tail.own()
    tail.back()
    tail.spread()
    big.end()
    tail.end()
    net.put("sib", oa_ref, ob_ref, at.sib)
    net.got("sib")
    net.finish()


def layer_call(length, tokens, cotangent, qkv, out_w, up_w, down_w, vec, vec_up, qvb):
    V = pltpu.VMEM
    sds = jax.ShapeDtypeStruct
    scratch = [
        V((512, 768), BF16), V((512, 768), BF16), V((512, 768), BF16), V((512, 768), F32), V((512, 128), F32),
        V((576, 768), BF16), V((576, 512), BF16), V((768, 512), BF16), V((3, 512, 512), F32), V((768, 768), BF16),
        V((384, 1536), BF16), V((384, 1536), BF16),
        V((512, 768), F32), V((512, 768), F32), V((512, 128), F32), V((512, 768), BF16), V((384, 512), BF16),
        V((384, 512), BF16), V((512, 1536), BF16), V((512, 1536), BF16), V((512, 768), BF16), V((512, 768), BF16),
        V((256, 384), F32), V((256, 384), F32), V((512, 768), F32), V((512, 768), BF16), V((32, 1536), F32),
        V((S_ROWS, 128), F32), V((192, 512), BF16), V((576, 512), BF16),
        V((16, 768), F32), V((16, 768), F32), V((16, 768), F32), V((16, 768), F32),
        V((512, 768), F32), V((256, 768), BF16), V((256, 768), BF16), V((256, 768), BF16), V((256, 768), BF16),
        V((9216, 128), BF16), V((5120, 128), BF16),
        V((2, 3, 1152, 128), BF16), V((2, 1152, 128), BF16), V((2, 3, 288, 128), BF16), V((2, 288, 128), BF16), V((288, 128), BF16),
        V((2, 3, 640, 128), BF16), V((2, 640, 128), BF16), V((2, 3, 160, 128), BF16), V((2, 160, 128), BF16), V((160, 128), BF16),
        pltpu.SemaphoreType.DMA((96,)), pltpu.SemaphoreType.DMA((96,)),
    ]
    vm = pl.BlockSpec(memory_space=V)
    return pl.pallas_call(
        layer_kernel,
        out_shape=(sds((256, 384), BF16), sds((256, 768), F32), sds((9216, 128), BF16), sds((5120, 128), BF16),
                   sds((5120, 128), BF16)),
        in_specs=[pl.BlockSpec(memory_space=pltpu.SMEM)] + [vm] * 9,
        out_specs=(vm,) * 5,
        scratch_shapes=scratch,
        compiler_params=pltpu.CompilerParams(collective_id=0, has_side_effects=True, vmem_limit_bytes=60 << 20),
        name="layer",
    )(length, tokens, cotangent, qkv, out_w, up_w, down_w, vec, vec_up, qvb)


def per_device(tokens, seq_lengths, cotangent, qkv_weight, qv_bias, out_weight, out_bias,
               first_gain, first_shift, second_gain, second_shift, up_weight, up_bias, down_weight, down_bias):
    j = lax.axis_index("grid")
    own = lax.dynamic_slice_in_dim(qv_bias, 192 * j, 192, 1)
    qvb = jnp.broadcast_to(own.reshape(384, 1), (384, 512))
    rows = [out_bias, first_gain, first_shift, second_gain, second_shift, jnp.zeros_like(out_bias),
            jnp.pad(down_bias, (0, 384)), jnp.zeros_like(out_bias)]
    lo, ig, om, oa, ob = layer_call(
        seq_lengths, tokens, cotangent, qkv_weight, out_weight, up_weight, down_weight,
        jnp.stack(rows), up_bias.reshape(1, -1), qvb)
    return finish(lo, ig, om, oa, ob, j)


def finish(lo, ig, om, oa, ob, j):
    first = jnp.where(j == 0, oa, ob).astype(F32)
    second = jnp.where(j == 0, ob, oa).astype(F32)
    mlp = om.astype(F32).reshape(2, 12, 384, 128).transpose(0, 2, 1, 3).reshape(2, 384, 1536)
    qkv = [a[:3456].reshape(6, 3, 192, 128).transpose(1, 2, 0, 3).reshape(3, 192, 768) for a in (first, second)]
    outw = [a[3456:4608].reshape(6, 192, 128).transpose(1, 0, 2).reshape(192, 768) for a in (first, second)]
    sm = oa[4608 : 4608 + S_ROWS].astype(F32)
    bias = [a[4608 : 4608 + 4].reshape(2, 256)[:, :192] for a in (first, second)]
    row = lambda at, n: sm[at : at + n].reshape(-1)
    return (
        lo, ig, jnp.concatenate(qkv, axis=1), jnp.concatenate(bias, axis=1), jnp.concatenate(outw, axis=0),
        row(S_OB, 6), row(S_G1, 6), row(S_H1, 6), row(S_G2, 6), row(S_H2, 6),
        mlp[0], row(S_UB, 12), mlp[1], row(S_DB, 3),
    )
def solution(mesh):
    placed = (
        P(("dp", "grid"), None), P("dp"), P(("dp", "grid"), None), P(None, "mp", None), P(None, "mp"),
        P("mp", None), P(), P(), P(), P(), P(), P("mp", "grid"), P("grid"), P("mp", "grid"), P("mp"),
    )
    return jax.shard_map(
        per_device,
        mesh=mesh,
        in_specs=placed,
        out_specs=(
            P(("dp", "grid"), "mp"), P(("dp", "grid"), None), P(None, "mp", None), P(None, "mp"), P("mp", None),
            P(), P(), P(), P(), P(), P("mp", "grid"), P("grid"), P("mp", "grid"), P("mp"),
        ),
        check_vma=False,
    )
```

time: 367 us -> 194 us (0.53)
  waiting for transfers between devices: 125 us -> 0 us
  Pallas kernels: 58.7 us -> 147 us
  matrix products: 47.3 us -> 0 us
  blocking collectives: 37.4 us -> 0 us
  other arithmetic: 28.4 us -> 8.7 us
  local copies, waits for them, and re-layouts: 52.1 us -> 35.9 us
  between operations: 15.8 us -> 1.39 us
    pallas_call x1, Pallas kernels: 58.7 us -> 147 us  [layer_call(): pl.pallas_call(layer_kernel, out_shape=(sds((256, 384), BF16), sds((256,...]
    all_gather x4 -> x0, waiting for transfers between devices: 72.6 us -> none  [the longest x1 36.3 us: per_device(): down_all = lax.all_gather(down_weight, 'mp', axis=0, tiled=True)]
    psum x2 -> x0, waiting for transfers between devices: 50.6 us -> none  [the longest x1 27.3 us: per_device(): gn2 = lax.psum(dot(grad_pre, up_all, 1, 1), 'grid')]
    dot_general x36 -> x0, matrix products: 47.3 us -> none  [dot(): lax.dot_general(left, right, (((left_dim,), (right_dim,)), ((), ())), pre...]
    all_gather x5 -> x0, blocking collectives: 32 us -> none  [the longest x1 13.9 us: per_device(): att_all = lax.all_gather(att, ('mp', 'grid'), axis=1, tiled=True)]
    unnamed x177 -> x14, local copies, waits for them, and re-layouts: 24.2 us -> 8.06 us
    convert_element_type x7 -> x2, other arithmetic: 13.4 us -> 2.78 us  [the longest x1 2.05 us: finish(): first = jnp.where(j == 0, oa, ob).astype(F32)]
    reduce_sum x10 -> x0, other arithmetic: 9.78 us -> none  [the longest x1 2.86 us: per_device(): g2gain = jnp.sum(gn2 * n2, axis=0)]
  transfers between devices with their start and end apart: 8 -> 0, of which waited for: 4 -> 0; matrix products, arithmetic and copies ran while one was open for 24% -> 0% of each run, Pallas kernels for 16% -> 0%
where the time goes in v2:
time: 194 us; the launch traced here: 193 us
  Pallas kernels  147 us (76%)
  local copies, waits for them, and re-layouts  35.9 us (19%)
  other arithmetic  8.7 us (4%)
    pallas_call x1, Pallas kernels, layer_call(): pl.pallas_call(layer_kernel, out_shape=(sds((256, 384), BF16), sds((256,...  147 us
    unnamed x14, local copies, waits for them, and re-layouts  8.06 us
    reshape x4, local copies, waits for them, and re-layouts, finish(): a[:3456].reshape(6, 3, 192, 128).transpose(1, 2, 0, 3).reshape(3, 192, 768)  7.78 us
    concatenate x1, other arithmetic, finish(): jnp.concatenate(qkv, axis=1)  4.18 us
    slice x1, local copies, waits for them, and re-layouts, finish(): mlp[1]  4.18 us
    another operation x7, local copies, waits for them, and re-layouts, per_device(): jnp.stack(rows)  4.1 us

profile of v2, /device:TPU:1, one launch (start us, length us, event | category | flops | bytes accessed | tf_op | source)
XLA Modules:
  0.0 193.4 jit_solution(15934020690859374586)
XLA Ops:
  0.6 0.0 copy-start
  1.3 0.0 copy-done
  1.3 0.1 constant_dynamic-slice_fusion
  1.4 0.1 broadcast_in_dim.7
  1.5 0.7 stack.21
  2.2 0.7 stack.22
  2.9 0.7 stack.23
  3.6 0.7 stack.24
  4.3 0.7 stack.25
  4.9 0.7 pad.4
  5.6 0.7 stack.27.vec
  6.3 1.3 reshape.93.vec_up
  7.6 1.0 broadcast_in_dim.8.qvb
  8.6 147.4 %layer.1 = (bf16[256,384]{1,0:T(8,128)(2,1)}, f32[256,768]{1,0:T(8,128)}, bf16[9216,128]{1,0:T(8,128)(2,1)}, bf16[5120,128]{1,0:T(8,128)(2,1)}, bf16[5120,128]{1,0:T(8,128)(2,1)}) custom-call(s32[1]{0:T(128)S(6)} %copy.52.length_ref, bf16[256,768]{1,0:T(8,128)(2,1)} %tokens.1, bf16[256,768]{1,0:T(8,128)(2,1)} %cotangent.1, bf16[3,384,768]{2,1,0:T(8,128)(2,1)} %qkv_ref.1, ...), custom_call_target="tpu_custom_call" | custom-call | tf_op jit(solution)/shard_map/layer/pallas_call | solution.py:457
  156.0 0.7 slice_convert_fusion
  156.7 0.6 slice_bitcast_fusion.6
  157.3 0.6 slice_bitcast_fusion
  157.9 0.6 slice_bitcast_fusion.1
  158.5 2.1 %select_convert_fusion.1 = (f32[5120,128]{1,0:T(8,128)S(1)}, f32[5120,128]{1,0:T(8,128)S(1)}) fusion(bf16[5120,128]{1,0:T(8,128)(2,1)} %get-tuple-element.21, bf16[5120,128]{1,0:T(8,128)(2,1)} %get-tuple-element.22, pred[]{:T(512)S(6)} %eq.4), kind=kLoop, calls=%fused_computation.4 | loop fusion | flops 2621440 | bytes 7864321 | tf_op jit(solution)/shard_map/convert_element_type | solution.py:483
  160.6 0.0 copy-start.1
  160.6 1.5 copy-done.1
  162.1 0.7 pad_maximum_fusion.2
  162.8 1.1 slice.80
  163.9 1.6 slice.74
  165.5 0.4 copy.37
  165.8 2.4 %copy.49 = f32[6,3,192,128]{3,0,2,1:T(8,128)} copy(f32[6,3,192,128]{3,2,1,0:T(8,128)S(1)} %bitcast.45) | data formatting | bytes 3538944 | tf_op jit(solution)/shard_map/reshape | solution.py:486
  168.2 2.7 %reshape.95 = f32[3,192,768]{2,1,0:T(8,128)} reshape(f32[3,192,6,128]{3,2,1,0:T(8,128)} %bitcast.42) | data formatting | bytes 3538944 | tf_op jit(solution)/shard_map/reshape | solution.py:486
  171.0 0.1 slice.75
  171.1 0.4 copy.38
  171.5 0.3 copy_bitcast_fusion.2
  171.8 1.1 pad_maximum_fusion.1
  172.9 1.0 copy.48
  173.9 1.6 reshape.97
  175.5 0.0 copy-start.2
  175.5 4.2 %pad_maximum_fusion = f32[3,384,768]{2,1,0:T(8,128)} fusion(f32[3,192,768]{2,1,0:T(8,128)} %reshape.97, f32[3,192,768]{2,1,0:T(8,128)} %reshape.95), kind=kLoop, calls=%fused_computation | loop fusion | flops 884736 | bytes 7077888 | tf_op jit(solution)/shard_map/concatenate | solution.py:492
  179.7 0.0 copy-done.2
  179.7 3.0 %copy.39 = f32[2,12,384,128]{2,3,1,0:T(8,128)} copy(bf16[2,12,384,128]{3,2,1,0:T(8,128)(2,1)S(1)} %bitcast.48) | data formatting | bytes 7077888 | tf_op jit(solution)/shard_map/transpose | solution.py:485
  182.6 4.2 %fusion = (f32[1,384,12,128]{1,3,2,0:T(8,128)}, f32[1,384,12,128]{1,3,2,0:T(8,128)S(1)}) fusion(f32[2,384,12,128]{1,3,2,0:T(8,128)} %bitcast.39), kind=kLoop, calls=%fused_computation.18 | loop fusion | bytes 9437184 | tf_op jit(solution)/shard_map/slice | solution.py:494
  186.8 3.0 %copy.41 = f32[384,1536]{1,0:T(8,128)} copy(f32[384,1536]{0,1:T(8,128)} %bitcast.41) | data formatting | bytes 4718592
  189.9 0.0 copy-start.4
  189.9 0.0 copy-start.3
  189.9 1.9 %copy.40 = f32[384,1536]{1,0:T(8,128)} copy(f32[384,1536]{0,1:T(8,128)S(1)} %bitcast.40) | data formatting | bytes 4718592
  191.8 0.0 copy-done.4
  191.8 0.7 copy.53
  192.5 0.0 copy-done.3
  192.5 0.9 copy.54
  (7 shorter events, 0.1 us)
Async XLA Ops:
  0.6 0.7 copy-start
  160.6 1.5 copy-start.1
  175.5 4.2 %copy-start.2 = (bf16[9216,128]{1,0:T(8,128)(2,1)S(1)}, bf16[9216,128]{1,0:T(8,128)(2,1)}, u32[]{:S(2)}) copy-start(bf16[9216,128]{1,0:T(8,128)(2,1)} %get-tuple-element.23) | copy-start | bytes 7077892
  189.9 1.9 %copy-start.4 = (bf16[256,384]{1,0:T(8,128)(2,1)S(1)}, bf16[256,384]{1,0:T(8,128)(2,1)}, u32[]{:S(2)}) copy-start(bf16[256,384]{1,0:T(8,128)(2,1)} %get-tuple-element.63) | copy-start | bytes 589828
  189.9 2.6 %copy-start.3 = (f32[256,768]{1,0:T(8,128)S(1)}, f32[256,768]{1,0:T(8,128)}, u32[]{:S(2)}) copy-start(f32[256,768]{1,0:T(8,128)} %get-tuple-element.64) | copy-start | bytes 2359300

commit v3 on v2

--- a/solution.py
+++ b/solution.py
@@ -37,14 +37,16 @@
         self.xa = {"mp": 1 - self.i}
         self.xb = {"dp": dp + 1 - 2 * self.xh, "mp": 1 - self.i}
         self.xc = {"mp": 1 - self.i, "grid": 1 - self.j}
-        self.far = {"dp": dp + 1 - 2 * self.xh}
-        self.ring = (
-            [{"dp": dp + 2 * (lax.rem(self.y + d, 4) - self.y)} for d in (1, 2, 3)],
-            [{"dp": dp + 8 * (lax.rem(self.z + d, 4) - self.z)} for d in (1, 2, 3)],
+        steps = (
+            [2 * (lax.rem(self.y + d, 4) - self.y) for d in range(4)],
+            [8 * (lax.rem(self.z + d, 4) - self.z) for d in range(4)],
         )
+        flip = [0, 1 - 2 * self.xh]
+        self.ring = [[{"dp": dp + r[d]} for d in (1, 2, 3)] for r in steps]
+        self.eight = [[{"dp": dp + r[k // 2] + flip[k % 2]} for k in range(8)] for r in steps]
 
     def all(self):
-        return [self.sib, self.xa, self.xb, self.xc, self.far] + self.ring[0] + self.ring[1]
+        return [self.sib, self.xa, self.xb, self.xc] + self.eight[0][1:] + self.eight[1][2:]
 
 
 class Copies:
@@ -68,13 +70,14 @@
 
 
 class Reduce:
-    def __init__(self, tag, net, at, src, out, r1, p1, r2, p2, rx):
+    def __init__(self, tag, net, at, src, out, r1, p1, r2):
         self.tag, self.net, self.at = tag, net, at
-        self.src, self.out, self.r1, self.p1, self.r2, self.p2, self.rx = src, out, r1, p1, r2, p2, rx
+        self.src, self.out, self.r1, self.p1, self.r2 = src, out, r1, p1, r2
         self.half = src.shape[0] // 2
-        self.big, self.small = self.half // 4, self.half // 16
+        self.big, self.small = self.half // 4, self.half // 32
         self.pos = ((at.y, at.z), (at.z, at.y))
-        self.rings = ((at.ring[0], at.ring[1]), (at.ring[1], at.ring[0]))
+        self.rings = ((at.ring[0],), (at.ring[1],))
+        self.eights = (at.eight[1], at.eight[0])
 
     def start(self, s):
         for d in (1, 2, 3):
@@ -82,60 +85,49 @@
             self.net.put((self.tag, 1, s, d), self.src.at[pl.ds(up16(s * self.half + to * self.big), self.big)],
                          self.r1.at[s, d - 1], self.rings[s][0][d - 1])
 
+    def part(self, s, k):
+        across = self.at.xh + (k % 2) * (1 - 2 * self.at.xh)
+        return (2 * lax.rem(self.pos[s][1] + k // 2, 4) + across) * self.small
+
     def second(self, s):
         base = s * self.half + self.pos[s][0] * self.big
         for d in (1, 2, 3):
             self.net.got((self.tag, 1, s, d))
-        for d in (1, 2, 3, 0):
-            off = lax.rem(self.pos[s][1] + d, 4) * self.small
+        for k in (1, 2, 3, 4, 5, 6, 7, 0):
+            off = self.part(s, k)
             rows = pl.ds(up16(off), self.small)
             total = self.src[pl.ds(up16(base + off), self.small), :].astype(F32)
             for e in range(3):
                 total = total + self.r1[s, e, rows, :].astype(F32)
             self.p1[s, rows, :] = total.astype(BF16)
-            if d:
-                self.net.put((self.tag, 2, s, d), self.p1.at[s, rows], self.r2.at[s, d - 1], self.rings[s][1][d - 1])
-
-    def third(self):
-        for s in (0, 1):
-            rows = pl.ds(up16(self.pos[s][1] * self.small), self.small)
-            for d in (1, 2, 3):
-                self.net.got((self.tag, 2, s, d))
-            total = self.p1[s, rows, :].astype(F32)
-            for e in range(3):
-                total = total + self.r2[s, e].astype(F32)
-            self.p2[s] = total.astype(BF16)
-        self.net.put((self.tag, 3), self.p2.at[1 - self.at.xh], self.rx, self.at.far)
+            if k:
+                self.net.put((self.tag, 2, s, k), self.p1.at[s, rows], self.r2.at[s, k - 1], self.eights[s][k])
 
     def place(self, s):
-        return s * self.half + self.pos[s][0] * self.big + self.pos[s][1] * self.small
-
-    def own(self):
-        self.net.got((self.tag, 3))
-        where = up16(self.place(0) + self.at.xh * (self.place(1) - self.place(0)))
-        rows = pl.ds(where, self.small)
-        self.out[rows, :] = (self.p2[self.at.xh].astype(F32) + self.rx[...].astype(F32)).astype(BF16)
-        self.net.put((self.tag, 4), self.out.at[rows], self.out.at[rows], self.at.far)
-
-    def back(self):
-        self.net.got((self.tag, 4))
-        for s in (0, 1):
-            rows = pl.ds(up16(self.place(s)), self.small)
-            for d in (1, 2, 3):
-                self.net.put((self.tag, 5, s, d), self.out.at[rows], self.out.at[rows], self.rings[s][1][d - 1])
-
-    def spread(self):
-        for s in (0, 1):
-            rows = pl.ds(up16(s * self.half + self.pos[s][0] * self.big), self.big)
-            for d in (1, 2, 3):
-                self.net.got((self.tag, 5, s, d))
-            for d in (1, 2, 3):
-                self.net.put((self.tag, 6, s, d), self.out.at[rows], self.out.at[rows], self.rings[s][0][d - 1])
+        return pl.ds(up16(s * self.half + self.pos[s][0] * self.big + self.part(s, 0)), self.small)
+
+    def own(self, s):
+        for k in range(1, 8):
+            self.net.got((self.tag, 2, s, k))
+        total = self.p1[s, pl.ds(up16(self.part(s, 0)), self.small), :].astype(F32)
+        for e in range(7):
+            total = total + self.r2[s, e].astype(F32)
+        rows = self.place(s)
+        self.out[rows, :] = total.astype(BF16)
+        for k in range(1, 8):
+            self.net.put((self.tag, 3, s, k), self.out.at[rows], self.out.at[rows], self.eights[s][k])
+
+    def spread(self, s):
+        rows = pl.ds(up16(s * self.half + self.pos[s][0] * self.big), self.big)
+        for k in range(1, 8):
+            self.net.got((self.tag, 3, s, k))
+        for d in (1, 2, 3):
+            self.net.put((self.tag, 4, s, d), self.out.at[rows], self.out.at[rows], self.rings[s][0][d - 1])
 
     def end(self):
         for s in (0, 1):
             for d in (1, 2, 3):
-                self.net.got((self.tag, 6, s, d))
+                self.net.got((self.tag, 4, s, d))
 
 
 def column_sum8(values):
@@ -147,12 +139,13 @@
 
 
 def layer_kernel(
-    length_ref, tokens, cotangent, qkv_ref, out_ref, up_ref, down_ref, vec, vec_up, qvb,
+    length_ref, tokens, cotangent, qkv_ref, out_ref, up_ref, down_ref, qvb_in, ob_in, g1_in, h1_in, g2_in, h2_in,
+    ub_in, db_in,
     lo_ref, ig_ref, om_ref, oa_ref, ob_ref,
     x_all, cot, normed1, n1, scale1, wown, qkvt, attt, probs, out_all, up_oth, down_oth,
     h1, n2, scale2, normed2, n2t, cott, hid, gpre, gn, gn_sib, mo, mo_sib, gh1, gb, acc, small, gattt, gt,
     g1_own, g1_sib, g1_sum, g1_far, gn1_keep, gn1_out, gn1_in, gn1_mine, gn1_far,
-    gm, ga, m1, mp1, m2, mp2, mx, a1, ap1, a2, ap2, ax, send, recv,
+    gm, ga, m1, mp1, m2, a1, ap1, a2, vec, vec_up, send, recv,
 ):
     at = Place()
     i, j = at.i, at.j
@@ -169,12 +162,34 @@
     net.put("tok", tokens, x_all.at[mine], at.sib)
     net.put("cot", cotangent, cot.at[mine], at.sib)
     for n, peer in enumerate((at.xa, at.xb)):
-        part = pl.ds(192 * n, 192)
-        net.put(("out", n), out_ref.at[part], out_all.at[pl.ds(up16(384 * i + 192 * n), 192)], peer)
-    for name, src, dst in (("up", up_ref, up_oth), ("down", down_ref, down_oth)):
-        for n, peer in enumerate((at.xa, at.xb)):
-            part = pl.ds(192 * n, 192)
-            net.put((name, n), src.at[part], dst.at[part], peer)
+        part = 192 * j + 96 * n
+        net.put(("out", n), out_ref.at[pl.ds(up16(part), 96)], out_all.at[pl.ds(up16(384 * i + part), 96)], peer)
+    odd_y, odd_z = lax.rem(at.y, 2), lax.rem(at.z, 2)
+    quarter = 2 * odd_y + odd_z
+    weights = (("up", up_ref, up_oth), ("down", down_ref, down_oth))
+
+    def weight_rows(q, n):
+        return pl.ds(up16(96 * q + 48 * n), 48)
+
+    for way, q in (("x", quarter), ("w", 3 - quarter)):
+        for name, src, dst in weights:
+            for n, peer in enumerate((at.xa, at.xb)):
+                net.put((name, way, n), src.at[weight_rows(q, n)], dst.at[weight_rows(q, n)], peer)
+
+    def pass_on(which):
+        name, _, dst = weights[which]
+        for n in range(2):
+            net.got((name, "x", n))
+        for axis in range(2):
+            for n in range(2):
+                rows = weight_rows(quarter, n)
+                net.put((name, axis, n), dst.at[rows], dst.at[rows], at.ring[axis][2 * n])
+
+    def weight_here(which):
+        name = weights[which][0]
+        for way in ("w", 0, 1):
+            for n in range(2):
+                net.got((name, way, n))
 
     x_all[mine, :] = tokens[...]
     cot[mine, :] = cotangent[...]
@@ -194,18 +209,33 @@
             scale1[rows, :] = jnp.broadcast_to(sc, (64, 128))
             normed1[rows, :] = (n * vec[V_G1 : V_G1 + 1, :] + vec[V_H1 : V_H1 + 1, :]).astype(BF16)
 
+    for n, ref in enumerate((ob_in, g1_in, h1_in, g2_in, h2_in)):
+        vec[n : n + 1, :] = ref[...].reshape(1, 768)
+    vec[V_DB : V_DB + 1, 0:384] = db_in[...].reshape(1, 384)
+    vec_up[...] = ub_in[...].reshape(1, 1536)
     first_norm(256 * j)
     net.got("tok")
     first_norm(256 * (1 - j))
 
+    ones = jnp.ones((16, 512), BF16)
+    line = lax.broadcasted_iota(jnp.int32, (16, 192), 0)
+
+    def bias_columns(n):
+        b = jnp.where(j == 0, qvb_in[n : n + 1, 0:192], qvb_in[n : n + 1, 192:384])
+        t1 = b.astype(BF16).astype(F32)
+        t2 = (b - t1).astype(BF16).astype(F32)
+        terms = jnp.where(line == 0, t1, jnp.where(line == 1, t2, jnp.where(line == 2, b - t1 - t2, 0.0)))
+        return dot(terms.astype(BF16), ones, 0, 0)
+
     for t in range(3):
         r = dot(wown[192 * t : 192 * t + 192, :], normed1[...], 1, 1)
         if t == 0:
-            r = (r + qvb[0:192, :]).astype(BF16).astype(F32) * (HD**-0.5)
+            r = (r + bias_columns(0)).astype(BF16).astype(F32) * (HD**-0.5)
         if t == 2:
-            r = r + qvb[192:384, :]
+            r = r + bias_columns(1)
         qkvt[192 * t : 192 * t + 192, :] = r.astype(BF16)
 
+    pass_on(0)
     length = length_ref[0]
     own_rows = 384 * i + 192 * j
     for h in range(3):
@@ -225,6 +255,13 @@
         rows = pl.ds(up16(own_rows + 64 * h), 64)
         for n, peer in enumerate((at.xc, at.xa, at.sib)):
             net.put(("att", h, n), attt.at[rows], attt.at[rows], peer)
+        if h == 0:
+            pass_on(1)
+        if h == 1:
+            for n in range(2):
+                net.got(("out", n))
+            far_rows = pl.ds(up16(384 * (1 - i) + 192 * j), 192)
+            net.put("outs", out_all.at[far_rows], out_all.at[far_rows], at.sib)
 
     net.got("cot")
     cott[...] = cot[:, ipart].T
@@ -235,8 +272,7 @@
             small[row + c : row + c + 1, :] = value[:, 128 * c : 128 * c + 128]
 
     put_small(S_DB, jnp.sum(cot[:, ipart].astype(F32), axis=0, keepdims=True))
-    for n in range(2):
-        net.got(("out", n))
+    net.got("outs")
     for h in range(3):
         for n in range(3):
             net.got(("att", h, n))
@@ -255,9 +291,8 @@
         normed2[rows, :] = (n * vec[V_G2 : V_G2 + 1, :] + vec[V_H2 : V_H2 + 1, :]).astype(BF16)
 
     n2t[...] = normed2[:, ipart].T
-    for name in ("up", "down"):
-        for n in range(2):
-            net.got((name, n))
+    weight_here(0)
+    weight_here(1)
 
     @pl.loop(0, 6)
     def _(c):
@@ -282,7 +317,7 @@
         gn[rows, opart] = dot(gpre[rows, :], up_oth[...], 1, 1).astype(BF16)
         net.put(("gn", c), gn.at[rows], gn_sib.at[rows], at.sib)
 
-    big = Reduce("m", net, at, gm, om_ref, m1, mp1, m2, mp2, mx)
+    big = Reduce("m", net, at, gm, om_ref, m1, mp1, m2)
     for s, left, right in ((1, cott, hid), (0, n2t, gpre)):
         @pl.loop(0, 6)
         def _(c):
@@ -342,13 +377,10 @@
             rows = slice(base + 64 * h, base + 64 * h + 64)
             gt[rows, 0:256] = (parts[0] + parts[1][:, 0:256]).astype(BF16)
             gt[rows, 256:512] = parts[1][:, 256:512].astype(BF16)
-        if h == 0:
+        if h == 1:
             big.second(1)
+        if h == 2:
             big.second(0)
-        elif h == 1:
-            big.third()
-        else:
-            big.own()
 
     @pl.loop(0, 2)
     def _(b):
@@ -377,13 +409,20 @@
         g1_own[8 * n : 8 * n + 8, :] = jnp.broadcast_to(
             jnp.sum(acc[8 * n : 8 * n + 8, 0:768], axis=0, keepdims=True), (8, 768))
     net.put("g1", g1_own, g1_sib, at.sib)
-    big.back()
-
-    ones = jnp.ones((16, 512), BF16)
+    big.own(1)
+
     for base, row in ((0, S_QB), (384, S_VB)):
         r = dot(ones, gt[base : base + 192, :], 1, 1)
         small[row : row + 1, :] = r[0:1, 0:128]
         small[row + 1 : row + 2, 0:64] = r[0:1, 128:192]
+    net.got("g1")
+    g1_sum[...] = g1_own[...] + g1_sib[...]
+    net.put("g1x", g1_sum, g1_far, at.xa)
+    net.got("gn1")
+    half_sum = gn1_keep[mine, :] + gn1_in[...].astype(F32)
+    gn1_mine[...] = half_sum.astype(BF16)
+    net.put("gn1x", gn1_mine, gn1_far, at.xa)
+    big.own(0)
     for n in range(3):
         r = dot(gt[192 * n : 192 * n + 192, :], normed1[...], 1, 0).astype(BF16)
         for c in range(6):
@@ -392,26 +431,19 @@
     for c in range(6):
         ga[pl.ds(3456 + 192 * c, 192), :] = r[:, 128 * c : 128 * c + 128]
     ga[pl.ds(4608 + S_ROWS, 512 - S_ROWS), :] = jnp.zeros((512 - S_ROWS, 128), BF16)
-    tail = Reduce("a", net, at, ga, oa_ref, a1, ap1, a2, ap2, ax)
+    tail = Reduce("a", net, at, ga, oa_ref, a1, ap1, a2)
     tail.start(0)
 
-    net.got("g1")
-    g1_sum[...] = g1_own[...] + g1_sib[...]
-    net.put("g1x", g1_sum, g1_far, at.xa)
-    net.got("gn1")
-    half_sum = gn1_keep[mine, :] + gn1_in[...].astype(F32)
-    gn1_mine[...] = half_sum.astype(BF16)
-    net.put("gn1x", gn1_mine, gn1_far, at.xa)
     net.got("g1x")
     g1_own_sum = g1_sum[...] + g1_far[...]
     put_small(S_G1, g1_own_sum[0:1, :])
     put_small(S_H1, g1_own_sum[8:9, :])
     ga[pl.ds(4608, S_ROWS), :] = small[...].astype(BF16)
     tail.start(1)
-    big.spread()
+    big.spread(1)
+    big.spread(0)
     tail.second(0)
     tail.second(1)
-    tail.third()
     net.got("gn1x")
 
     @pl.loop(0, 4)
@@ -425,9 +457,10 @@
         mn = jnp.mean(e * n, axis=-1, keepdims=True)
         ig_ref[rows, :] = gh1[full, :] + (e - m - n * mn) * scale1[full, 0:1]
 
-    tail.own()
-    tail.back()
-    tail.spread()
+    tail.own(0)
+    tail.own(1)
+    tail.spread(0)
+    tail.spread(1)
     big.end()
     tail.end()
     net.put("sib", oa_ref, ob_ref, at.sib)
@@ -435,7 +468,7 @@
     net.finish()
 
 
-def layer_call(length, tokens, cotangent, qkv, out_w, up_w, down_w, vec, vec_up, qvb):
+def layer_call(*args):
     V = pltpu.VMEM
     sds = jax.ShapeDtypeStruct
     scratch = [
@@ -449,50 +482,88 @@
         V((16, 768), F32), V((16, 768), F32), V((16, 768), F32), V((16, 768), F32),
         V((512, 768), F32), V((256, 768), BF16), V((256, 768), BF16), V((256, 768), BF16), V((256, 768), BF16),
         V((9216, 128), BF16), V((5120, 128), BF16),
-        V((2, 3, 1152, 128), BF16), V((2, 1152, 128), BF16), V((2, 3, 288, 128), BF16), V((2, 288, 128), BF16), V((288, 128), BF16),
-        V((2, 3, 640, 128), BF16), V((2, 640, 128), BF16), V((2, 3, 160, 128), BF16), V((2, 160, 128), BF16), V((160, 128), BF16),
-        pltpu.SemaphoreType.DMA((96,)), pltpu.SemaphoreType.DMA((96,)),
+        V((2, 3, 1152, 128), BF16), V((2, 1152, 128), BF16), V((2, 7, 144, 128), BF16),
+        V((2, 3, 640, 128), BF16), V((2, 640, 128), BF16), V((2, 7, 80, 128), BF16),
+        V((8, 768), F32), V((1, 1536), F32),
+        pltpu.SemaphoreType.DMA((160,)), pltpu.SemaphoreType.DMA((160,)),
     ]
     vm = pl.BlockSpec(memory_space=V)
     return pl.pallas_call(
         layer_kernel,
         out_shape=(sds((256, 384), BF16), sds((256, 768), F32), sds((9216, 128), BF16), sds((5120, 128), BF16),
                    sds((5120, 128), BF16)),
-        in_specs=[pl.BlockSpec(memory_space=pltpu.SMEM)] + [vm] * 9,
+        in_specs=[pl.BlockSpec(memory_space=pltpu.SMEM)] + [vm] * 14,
         out_specs=(vm,) * 5,
         scratch_shapes=scratch,
         compiler_params=pltpu.CompilerParams(collective_id=0, has_side_effects=True, vmem_limit_bytes=60 << 20),
         name="layer",
-    )(length, tokens, cotangent, qkv, out_w, up_w, down_w, vec, vec_up, qvb)
+    )(*args)
+
+
+def finish_kernel(lo, ig, om, oa, ob, lo_out, ig_out, qkv_out, qvb_out, ow_out, out_bias, gain1, shift1, gain2, shift2,
+                  up_out, up_bias, down_out, down_bias, qkv, ow, up, down, sems):
+    j = lax.axis_index("grid")
+    copies = []
+
+    def send(src, dst):
+        copy = pltpu.make_async_copy(src, dst, sems.at[len(copies)])
+        copy.start()
+        copies.append(copy)
+
+    send(lo, lo_out)
+    send(ig, ig_out)
+    for s, scr, dst in ((0, up, up_out), (1, down, down_out)):
+        for c in range(12):
+            scr[:, 128 * c : 128 * c + 128] = om[4608 * s + 384 * c : 4608 * s + 384 * c + 384, :].astype(F32)
+        send(scr, dst)
+    for src, side in ((oa, j), (ob, 1 - j)):
+        rows = pl.ds(pl.multiple_of(192 * side, 192), 192)
+        for c in range(6):
+            ow[rows, 128 * c : 128 * c + 128] = src[3456 + 192 * c : 3648 + 192 * c, :].astype(F32)
+    send(ow, ow_out)
+    for n in range(3):
+        for src, side in ((oa, j), (ob, 1 - j)):
+            rows = pl.ds(pl.multiple_of(192 * side, 192), 192)
+            for c in range(6):
+                at = 576 * c + 192 * n
+                qkv[n, rows, 128 * c : 128 * c + 128] = src[at : at + 192, :].astype(F32)
+        send(qkv.at[n], qkv_out.at[n])
+    mine, other = (a[4608 : 4608 + S_ROWS, :].astype(F32) for a in (oa, ob))
+    first, second = jnp.where(j == 0, mine, other), jnp.where(j == 0, other, mine)
+    for n in range(2):
+        qvb_out[n : n + 1, :] = jnp.concatenate(
+            [part[2 * n + c : 2 * n + c + 1, : 128 - 64 * c] for part in (first, second) for c in range(2)], axis=1)
+    for dst, row, count in ((out_bias, S_OB, 6), (gain1, S_G1, 6), (shift1, S_H1, 6), (gain2, S_G2, 6),
+                            (shift2, S_H2, 6), (up_bias, S_UB, 12), (down_bias, S_DB, 3)):
+        for c in range(count):
+            dst[128 * c : 128 * c + 128] = mine[row + c]
+    for copy in copies:
+        copy.wait()
+
+
+def finish(*args):
+    V, hbm = pl.BlockSpec(memory_space=pltpu.VMEM), pl.BlockSpec(memory_space=pl.ANY)
+    f = lambda *shape: jax.ShapeDtypeStruct(shape, F32)
+    return pl.pallas_call(
+        finish_kernel,
+        out_shape=(jax.ShapeDtypeStruct((256, 384), BF16), f(256, 768), f(3, 384, 768), f(2, 384), f(384, 768),
+                   f(768), f(768), f(768), f(768), f(768), f(384, 1536), f(1536), f(384, 1536), f(384)),
+        in_specs=[hbm, hbm, V, V, V],
+        out_specs=(hbm, hbm, hbm, V, hbm, V, V, V, V, V, hbm, V, hbm, V),
+        scratch_shapes=[pltpu.VMEM((3, 384, 768), F32), pltpu.VMEM((384, 768), F32), pltpu.VMEM((384, 1536), F32),
+                        pltpu.VMEM((384, 1536), F32), pltpu.SemaphoreType.DMA((8,))],
+        compiler_params=pltpu.CompilerParams(vmem_limit_bytes=40 << 20),
+        name="finish",
+    )(*args)
 
 
 def per_device(tokens, seq_lengths, cotangent, qkv_weight, qv_bias, out_weight, out_bias,
                first_gain, first_shift, second_gain, second_shift, up_weight, up_bias, down_weight, down_bias):
-    j = lax.axis_index("grid")
-    own = lax.dynamic_slice_in_dim(qv_bias, 192 * j, 192, 1)
-    qvb = jnp.broadcast_to(own.reshape(384, 1), (384, 512))
-    rows = [out_bias, first_gain, first_shift, second_gain, second_shift, jnp.zeros_like(out_bias),
-            jnp.pad(down_bias, (0, 384)), jnp.zeros_like(out_bias)]
-    lo, ig, om, oa, ob = layer_call(
-        seq_lengths, tokens, cotangent, qkv_weight, out_weight, up_weight, down_weight,
-        jnp.stack(rows), up_bias.reshape(1, -1), qvb)
-    return finish(lo, ig, om, oa, ob, j)
-
-
-def finish(lo, ig, om, oa, ob, j):
-    first = jnp.where(j == 0, oa, ob).astype(F32)
-    second = jnp.where(j == 0, ob, oa).astype(F32)
-    mlp = om.astype(F32).reshape(2, 12, 384, 128).transpose(0, 2, 1, 3).reshape(2, 384, 1536)
-    qkv = [a[:3456].reshape(6, 3, 192, 128).transpose(1, 2, 0, 3).reshape(3, 192, 768) for a in (first, second)]
-    outw = [a[3456:4608].reshape(6, 192, 128).transpose(1, 0, 2).reshape(192, 768) for a in (first, second)]
-    sm = oa[4608 : 4608 + S_ROWS].astype(F32)
-    bias = [a[4608 : 4608 + 4].reshape(2, 256)[:, :192] for a in (first, second)]
-    row = lambda at, n: sm[at : at + n].reshape(-1)
-    return (
-        lo, ig, jnp.concatenate(qkv, axis=1), jnp.concatenate(bias, axis=1), jnp.concatenate(outw, axis=0),
-        row(S_OB, 6), row(S_G1, 6), row(S_H1, 6), row(S_G2, 6), row(S_H2, 6),
-        mlp[0], row(S_UB, 12), mlp[1], row(S_DB, 3),
-    )
+    return finish(*layer_call(
+        seq_lengths, tokens, cotangent, qkv_weight, out_weight, up_weight, down_weight, qv_bias, out_bias,
+        first_gain, first_shift, second_gain, second_shift, up_bias, down_bias))
+
+
 def solution(mesh):
     placed = (
         P(("dp", "grid"), None), P("dp"), P(("dp", "grid"), None), P(None, "mp", None), P(None, "mp"),

time: 194 us -> 138 us (0.71)
  local copies, waits for them, and re-layouts: 35.9 us -> 6.35 us
  Pallas kernels: 147 us -> 130 us
  other arithmetic: 8.7 us -> 0 us
    pallas_call x1, Pallas kernels: 147 us -> 126 us  [layer_call(): pl.pallas_call(layer_kernel, out_shape=(sds((256, 384), BF16), sds((256,...]
    reshape x13 -> x0, local copies, waits for them, and re-layouts: 11.9 us -> none  [the longest x4 7.78 us: finish(): a[:3456].reshape(6, 3, 192, 128).transpose(1, 2, 0, 3).reshape(3, 192, 768)]
    slice x7 -> x0, local copies, waits for them, and re-layouts: 7.03 us -> none  [the longest x1 4.18 us: finish(): mlp[1]]
    concatenate x3 -> x0, other arithmetic: 5.92 us -> none  [the longest x1 4.18 us: finish(): jnp.concatenate(qkv, axis=1)]
    pallas_call x0 -> x1, Pallas kernels: none -> 4.65 us  [finish(): pl.pallas_call(finish_kernel, out_shape=(jax.ShapeDtypeStruct((256, 384),...]
    another operation x8 -> x0, local copies, waits for them, and re-layouts: 4.11 us -> none  [the longest x7 4.1 us: per_device(): jnp.stack(rows)]
    transpose x1 -> x0, local copies, waits for them, and re-layouts: 2.98 us -> none  [finish(): om.astype(F32).reshape(2, 12, 384, 128).transpose(0, 2, 1, 3)]
    convert_element_type x2 -> x0, other arithmetic: 2.78 us -> none  [the longest x1 2.05 us: finish(): first = jnp.where(j == 0, oa, ob).astype(F32)]
where the time goes in v3:
time: 138 us
  Pallas kernels  130 us (94%)
  local copies, waits for them, and re-layouts  6.35 us (5%)
    pallas_call x1, Pallas kernels, layer_call(): pl.pallas_call(layer_kernel, out_shape=(sds((256, 384), BF16), sds((256,...  126 us
    unnamed x10, local copies, waits for them, and re-layouts  6.35 us
    pallas_call x1, Pallas kernels, finish(): pl.pallas_call(finish_kernel, out_shape=(jax.ShapeDtypeStruct((256, 384),...  4.65 us

profile of v3, /device:TPU:1, one launch (start us, length us, event | category | flops | bytes accessed | tf_op | source)
XLA Modules:
  0.0 138.1 jit_solution(4556118081710777554)
XLA Ops:
  1.3 125.7 %layer.1 = (bf16[256,384]{1,0:T(8,128)(2,1)}, f32[256,768]{1,0:T(8,128)}, bf16[9216,128]{1,0:T(8,128)(2,1)}, bf16[5120,128]{1,0:T(8,128)(2,1)}, bf16[5120,128]{1,0:T(8,128)(2,1)}) custom-call(s32[1]{0:T(128)S(6)} %copy.29.length_ref, bf16[256,768]{1,0:T(8,128)(2,1)} %tokens.1, bf16[256,768]{1,0:T(8,128)(2,1)} %cotangent.1, bf16[3,384,768]{2,1,0:T(8,128)(2,1)} %qkv_ref.1, ...), custom_call_target="tpu_custom_call" | custom-call | tf_op jit(solution)/shard_map/layer/pallas_call | solution.py:491
  127.0 0.0 copy-start
  127.1 1.7 %copy-done = bf16[9216,128]{1,0:T(8,128)(2,1)S(1)} copy-done((bf16[9216,128]{1,0:T(8,128)(2,1)S(1)}, bf16[9216,128]{1,0:T(8,128)(2,1)}, u32[]{:S(2)}) %copy-start) | copy-done | bytes 2359320
  128.7 0.0 copy-start.1
  128.7 1.3 copy-done.1
  130.0 0.0 copy-start.2
  130.0 1.3 copy-done.2
  131.3 0.0 copy-start.3
  131.3 1.1 copy-done.3
  132.5 0.0 copy-start.4
  132.5 0.9 copy-done.4
  133.4 4.6 %finish.1 = (bf16[256,384]{1,0:T(8,128)(2,1)}, f32[256,768]{1,0:T(8,128)}, f32[3,384,768]{2,1,0:T(8,128)}, f32[2,384]{1,0:T(2,128)}, f32[384,768]{1,0:T(8,128)},...) custom-call(bf16[256,384]{1,0:T(8,128)(2,1)S(1)} %copy-done.4, ...), custom_call_target="tpu_custom_call" | custom-call | tf_op jit(solution)/shard_map/finish/pallas_call | solution.py:547
Async XLA Ops:
  127.0 1.7 %copy-start = (bf16[9216,128]{1,0:T(8,128)(2,1)S(1)}, bf16[9216,128]{1,0:T(8,128)(2,1)}, u32[]{:S(2)}) copy-start(bf16[9216,128]{1,0:T(8,128)(2,1)} %get-tuple-element.21.om) | copy-start | bytes 7077892
  128.7 1.3 copy-start.1
  130.0 1.3 copy-start.2
  131.3 1.1 copy-start.3
  132.5 0.9 copy-start.4

commit v4 on v3

--- a/solution.py
+++ b/solution.py
@@ -36,7 +36,6 @@
         self.sib = {"grid": 1 - self.j}
         self.xa = {"mp": 1 - self.i}
         self.xb = {"dp": dp + 1 - 2 * self.xh, "mp": 1 - self.i}
-        self.xc = {"mp": 1 - self.i, "grid": 1 - self.j}
         steps = (
             [2 * (lax.rem(self.y + d, 4) - self.y) for d in range(4)],
             [8 * (lax.rem(self.z + d, 4) - self.z) for d in range(4)],
@@ -46,7 +45,7 @@
         self.eight = [[{"dp": dp + r[k // 2] + flip[k % 2]} for k in range(8)] for r in steps]
 
     def all(self):
-        return [self.sib, self.xa, self.xb, self.xc] + self.eight[0][1:] + self.eight[1][2:]
+        return [self.sib, self.xa, self.xb] + self.eight[0][1:] + self.eight[1][2:]
 
 
 class Copies:
@@ -161,20 +160,21 @@
 
     net.put("tok", tokens, x_all.at[mine], at.sib)
     net.put("cot", cotangent, cot.at[mine], at.sib)
+    odd_y, odd_z = lax.rem(at.y, 2), lax.rem(at.z, 2)
+    quarter = 2 * odd_y + odd_z
+    across = (quarter + 2 - 4 * odd_y, quarter + 1 - 2 * odd_z)
+    weights = (("up", up_ref, up_oth), ("down", down_ref, down_oth))
+
+    def weight_rows(q, start, size):
+        return pl.ds(up16(96 * q + start), size)
+
+    for name, src, dst in weights:
+        for n, peer in enumerate((at.xa, at.xb)):
+            rows = weight_rows(quarter, 48 * n, 48)
+            net.put((name, "x", n), src.at[rows], dst.at[rows], peer)
     for n, peer in enumerate((at.xa, at.xb)):
         part = 192 * j + 96 * n
         net.put(("out", n), out_ref.at[pl.ds(up16(part), 96)], out_all.at[pl.ds(up16(384 * i + part), 96)], peer)
-    odd_y, odd_z = lax.rem(at.y, 2), lax.rem(at.z, 2)
-    quarter = 2 * odd_y + odd_z
-    weights = (("up", up_ref, up_oth), ("down", down_ref, down_oth))
-
-    def weight_rows(q, n):
-        return pl.ds(up16(96 * q + 48 * n), 48)
-
-    for way, q in (("x", quarter), ("w", 3 - quarter)):
-        for name, src, dst in weights:
-            for n, peer in enumerate((at.xa, at.xb)):
-                net.put((name, way, n), src.at[weight_rows(q, n)], dst.at[weight_rows(q, n)], peer)
 
     def pass_on(which):
         name, _, dst = weights[which]
@@ -182,14 +182,23 @@
             net.got((name, "x", n))
         for axis in range(2):
             for n in range(2):
-                rows = weight_rows(quarter, n)
+                rows = weight_rows(quarter, 48 * n, 48)
                 net.put((name, axis, n), dst.at[rows], dst.at[rows], at.ring[axis][2 * n])
+
+    def pass_further(which):
+        name, _, dst = weights[which]
+        for axis in range(2):
+            net.got((name, 1 - axis, axis))
+            for n in range(2):
+                rows = weight_rows(across[1 - axis], 48 * axis + 32 * n, 32 - 16 * n)
+                net.put((name, "d", axis, n), dst.at[rows], dst.at[rows], at.ring[axis][2 * n])
 
     def weight_here(which):
         name = weights[which][0]
-        for way in ("w", 0, 1):
+        for axis in range(2):
+            net.got((name, axis, axis))
             for n in range(2):
-                net.got((name, way, n))
+                net.got((name, "d", axis, n))
 
     x_all[mine, :] = tokens[...]
     cot[mine, :] = cotangent[...]
@@ -253,15 +262,10 @@
             o = dot(qkvt[384 + 64 * h : 448 + 64 * h, 0:kr], p.astype(BF16), 1, 0)
             attt[pl.ds(up16(own_rows + 64 * h), 64), qc] = o.astype(BF16)
         rows = pl.ds(up16(own_rows + 64 * h), 64)
-        for n, peer in enumerate((at.xc, at.xa, at.sib)):
+        for n, peer in enumerate((at.xa, at.sib)):
             net.put(("att", h, n), attt.at[rows], attt.at[rows], peer)
-        if h == 0:
-            pass_on(1)
-        if h == 1:
-            for n in range(2):
-                net.got(("out", n))
-            far_rows = pl.ds(up16(384 * (1 - i) + 192 * j), 192)
-            net.put("outs", out_all.at[far_rows], out_all.at[far_rows], at.sib)
+
+    pass_on(1)
 
     net.got("cot")
     cott[...] = cot[:, ipart].T
@@ -272,9 +276,20 @@
             small[row + c : row + c + 1, :] = value[:, 128 * c : 128 * c + 128]
 
     put_small(S_DB, jnp.sum(cot[:, ipart].astype(F32), axis=0, keepdims=True))
+    far_rows = 384 * (1 - i) + 192 * j
+    pass_further(0)
+    for n in range(2):
+        net.got(("out", n))
+    rows = pl.ds(up16(far_rows), 192)
+    net.put("outs", out_all.at[rows], out_all.at[rows], at.sib)
+    pass_further(1)
+    for h in range(3):
+        net.got(("att", h, 0))
+        rows = pl.ds(up16(far_rows + 64 * h), 64)
+        net.put(("att", h, 2), attt.at[rows], attt.at[rows], at.sib)
     net.got("outs")
     for h in range(3):
-        for n in range(3):
+        for n in (1, 2):
             net.got(("att", h, n))
 
     @pl.loop(0, 4)
@@ -377,10 +392,6 @@
             rows = slice(base + 64 * h, base + 64 * h + 64)
             gt[rows, 0:256] = (parts[0] + parts[1][:, 0:256]).astype(BF16)
             gt[rows, 256:512] = parts[1][:, 256:512].astype(BF16)
-        if h == 1:
-            big.second(1)
-        if h == 2:
-            big.second(0)
 
     @pl.loop(0, 2)
     def _(b):
@@ -409,8 +420,6 @@
         g1_own[8 * n : 8 * n + 8, :] = jnp.broadcast_to(
             jnp.sum(acc[8 * n : 8 * n + 8, 0:768], axis=0, keepdims=True), (8, 768))
     net.put("g1", g1_own, g1_sib, at.sib)
-    big.own(1)
-
     for base, row in ((0, S_QB), (384, S_VB)):
         r = dot(ones, gt[base : base + 192, :], 1, 1)
         small[row : row + 1, :] = r[0:1, 0:128]
@@ -421,8 +430,6 @@
     net.got("gn1")
     half_sum = gn1_keep[mine, :] + gn1_in[...].astype(F32)
     gn1_mine[...] = half_sum.astype(BF16)
-    net.put("gn1x", gn1_mine, gn1_far, at.xa)
-    big.own(0)
     for n in range(3):
         r = dot(gt[192 * n : 192 * n + 192, :], normed1[...], 1, 0).astype(BF16)
         for c in range(6):
@@ -440,10 +447,19 @@
     put_small(S_H1, g1_own_sum[8:9, :])
     ga[pl.ds(4608, S_ROWS), :] = small[...].astype(BF16)
     tail.start(1)
+    big.second(1)
+    big.second(0)
+    tail.second(0)
+    tail.second(1)
+    big.own(1)
+    big.own(0)
+    tail.own(0)
+    tail.own(1)
+    net.put("gn1x", gn1_mine, gn1_far, at.xa)
     big.spread(1)
     big.spread(0)
-    tail.second(0)
-    tail.second(1)
+    tail.spread(0)
+    tail.spread(1)
     net.got("gn1x")
 
     @pl.loop(0, 4)
@@ -457,10 +473,6 @@
         mn = jnp.mean(e * n, axis=-1, keepdims=True)
         ig_ref[rows, :] = gh1[full, :] + (e - m - n * mn) * scale1[full, 0:1]
 
-    tail.own(0)
-    tail.own(1)
-    tail.spread(0)
-    tail.spread(1)
     big.end()
     tail.end()
     net.put("sib", oa_ref, ob_ref, at.sib)
@@ -500,10 +512,19 @@
     )(*args)
 
 
-def finish_kernel(lo, ig, om, oa, ob, lo_out, ig_out, qkv_out, qvb_out, ow_out, out_bias, gain1, shift1, gain2, shift2,
-                  up_out, up_bias, down_out, down_bias, qkv, ow, up, down, sems):
+def finish_kernel(lo, ig, om_in, oa_in, ob_in, lo_out, ig_out, qkv_out, qvb_out, ow_out, out_bias, gain1, shift1, gain2, shift2,
+                  up_out, up_bias, down_out, down_bias, qkv, ow, up, down, om, oa, ob,
+                  sems, in_sems):
     j = lax.axis_index("grid")
     copies = []
+    halves = [pl.ds(4608 * s, 4608) for s in range(2)]
+    fetch = [
+        pltpu.make_async_copy(src, dst, in_sems.at[n])
+        for n, (src, dst) in enumerate(
+            [(om_in.at[h], om.at[h]) for h in halves] + [(oa_in, oa), (ob_in, ob)])
+    ]
+    for copy in fetch:
+        copy.start()
 
     def send(src, dst):
         copy = pltpu.make_async_copy(src, dst, sems.at[len(copies)])
@@ -513,9 +534,12 @@
     send(lo, lo_out)
     send(ig, ig_out)
     for s, scr, dst in ((0, up, up_out), (1, down, down_out)):
+        fetch[s].wait()
         for c in range(12):
             scr[:, 128 * c : 128 * c + 128] = om[4608 * s + 384 * c : 4608 * s + 384 * c + 384, :].astype(F32)
         send(scr, dst)
+    fetch[2].wait()
+    fetch[3].wait()
     for src, side in ((oa, j), (ob, 1 - j)):
         rows = pl.ds(pl.multiple_of(192 * side, 192), 192)
         for c in range(6):
@@ -542,16 +566,17 @@
 
 
 def finish(*args):
-    V, hbm = pl.BlockSpec(memory_space=pltpu.VMEM), pl.BlockSpec(memory_space=pl.ANY)
+    V, hbm = pl.BlockSpec(memory_space=pltpu.VMEM), pl.BlockSpec(memory_space=pltpu.HBM)
     f = lambda *shape: jax.ShapeDtypeStruct(shape, F32)
     return pl.pallas_call(
         finish_kernel,
         out_shape=(jax.ShapeDtypeStruct((256, 384), BF16), f(256, 768), f(3, 384, 768), f(2, 384), f(384, 768),
                    f(768), f(768), f(768), f(768), f(768), f(384, 1536), f(1536), f(384, 1536), f(384)),
-        in_specs=[hbm, hbm, V, V, V],
+        in_specs=[hbm] * 5,
         out_specs=(hbm, hbm, hbm, V, hbm, V, V, V, V, V, hbm, V, hbm, V),
         scratch_shapes=[pltpu.VMEM((3, 384, 768), F32), pltpu.VMEM((384, 768), F32), pltpu.VMEM((384, 1536), F32),
-                        pltpu.VMEM((384, 1536), F32), pltpu.SemaphoreType.DMA((8,))],
+                        pltpu.VMEM((384, 1536), F32), pltpu.VMEM((9216, 128), BF16), pltpu.VMEM((5120, 128), BF16),
+                        pltpu.VMEM((5120, 128), BF16), pltpu.SemaphoreType.DMA((8,)), pltpu.SemaphoreType.DMA((4,))],
         compiler_params=pltpu.CompilerParams(vmem_limit_bytes=40 << 20),
         name="finish",
     )(*args)

time: 138 us -> 122 us (0.88)
  Pallas kernels: 130 us -> 114 us
    pallas_call x1, Pallas kernels: 126 us -> 109 us  [layer_call(): pl.pallas_call(layer_kernel, out_shape=(sds((256, 384), BF16), sds((256,...]
where the time goes in v4:
time: 122 us
  Pallas kernels  114 us (93%)
  local copies, waits for them, and re-layouts  6.35 us (5%)
  between operations  1.32 us (1%)
    pallas_call x1, Pallas kernels, layer_call(): pl.pallas_call(layer_kernel, out_shape=(sds((256, 384), BF16), sds((256,...  109 us
    unnamed x10, local copies, waits for them, and re-layouts  6.35 us
    pallas_call x1, Pallas kernels, finish(): pl.pallas_call(finish_kernel, out_shape=(jax.ShapeDtypeStruct((256, 384),...  5.4 us

profile of v4, /device:TPU:1, one launch (start us, length us, event | category | flops | bytes accessed | tf_op | source)
XLA Modules:
  0.0 121.8 jit_solution(16246354716001338679)
XLA Ops:
  1.3 108.8 %layer.1 = (bf16[256,384]{1,0:T(8,128)(2,1)}, f32[256,768]{1,0:T(8,128)}, bf16[9216,128]{1,0:T(8,128)(2,1)}, bf16[5120,128]{1,0:T(8,128)(2,1)}, bf16[5120,128]{1,0:T(8,128)(2,1)}) custom-call(s32[1]{0:T(128)S(6)} %copy.29.length_ref, bf16[256,768]{1,0:T(8,128)(2,1)} %tokens.1, bf16[256,768]{1,0:T(8,128)(2,1)} %cotangent.1, bf16[3,384,768]{2,1,0:T(8,128)(2,1)} %qkv_ref.1, ...), custom_call_target="tpu_custom_call" | custom-call | tf_op jit(solution)/shard_map/layer/pallas_call | solution.py:503
  110.1 0.0 copy-start
  110.1 1.7 %copy-done = bf16[9216,128]{1,0:T(8,128)(2,1)S(1)} copy-done((bf16[9216,128]{1,0:T(8,128)(2,1)S(1)}, bf16[9216,128]{1,0:T(8,128)(2,1)}, u32[]{:S(2)}) %copy-start) | copy-done | bytes 2359320
  111.8 0.0 copy-start.1
  111.8 1.3 %copy-done.1 = bf16[5120,128]{1,0:T(8,128)(2,1)S(1)} copy-done((bf16[5120,128]{1,0:T(8,128)(2,1)S(1)}, bf16[5120,128]{1,0:T(8,128)(2,1)}, u32[]{:S(2)}) %copy-start.1) | copy-done | bytes 1310744
  113.1 0.0 copy-start.2
  113.1 1.3 %copy-done.2 = bf16[5120,128]{1,0:T(8,128)(2,1)S(1)} copy-done((bf16[5120,128]{1,0:T(8,128)(2,1)S(1)}, bf16[5120,128]{1,0:T(8,128)(2,1)}, u32[]{:S(2)}) %copy-start.2) | copy-done | bytes 1310744
  114.4 0.0 copy-start.3
  114.4 1.1 copy-done.3
  115.5 0.0 copy-start.4
  115.5 0.9 copy-done.4
  116.4 5.4 %finish.1 = (bf16[256,384]{1,0:T(8,128)(2,1)}, f32[256,768]{1,0:T(8,128)}, f32[3,384,768]{2,1,0:T(8,128)}, f32[2,384]{1,0:T(2,128)}, f32[384,768]{1,0:T(8,128)},...) custom-call(bf16[256,384]{1,0:T(8,128)(2,1)S(1)} %copy-done.4, ...), custom_call_target="tpu_custom_call" | custom-call | tf_op jit(solution)/shard_map/finish/pallas_call | solution.py:571
Async XLA Ops:
  110.1 1.7 %copy-start = (bf16[9216,128]{1,0:T(8,128)(2,1)S(1)}, bf16[9216,128]{1,0:T(8,128)(2,1)}, u32[]{:S(2)}) copy-start(bf16[9216,128]{1,0:T(8,128)(2,1)} %get-tuple-element.21.om_in) | copy-start | bytes 7077892
  111.8 1.3 %copy-start.1 = (bf16[5120,128]{1,0:T(8,128)(2,1)S(1)}, bf16[5120,128]{1,0:T(8,128)(2,1)}, u32[]{:S(2)}) copy-start(bf16[5120,128]{1,0:T(8,128)(2,1)} %get-tuple-element.22.oa_in) | copy-start | bytes 3932164
  113.1 1.3 %copy-start.2 = (bf16[5120,128]{1,0:T(8,128)(2,1)S(1)}, bf16[5120,128]{1,0:T(8,128)(2,1)}, u32[]{:S(2)}) copy-start(bf16[5120,128]{1,0:T(8,128)(2,1)} %get-tuple-element.23.ob_in) | copy-start | bytes 3932164
  114.4 1.1 copy-start.3
  115.5 0.9 copy-start.4

commit v5 on v4

--- a/solution.py
+++ b/solution.py
@@ -69,8 +69,8 @@
 
 
 class Reduce:
-    def __init__(self, tag, net, at, src, out, r1, p1, r2):
-        self.tag, self.net, self.at = tag, net, at
+    def __init__(self, tag, net, at, src, out, r1, p1, r2, twin=None):
+        self.tag, self.net, self.at, self.twin = tag, net, at, twin
         self.src, self.out, self.r1, self.p1, self.r2 = src, out, r1, p1, r2
         self.half = src.shape[0] // 2
         self.big, self.small = self.half // 4, self.half // 32
@@ -116,17 +116,42 @@
         for k in range(1, 8):
             self.net.put((self.tag, 3, s, k), self.out.at[rows], self.out.at[rows], self.eights[s][k])
 
+    def piece(self, s, d, start, size):
+        to = lax.rem(self.pos[s][0] + d, 4)
+        return pl.ds(up16(s * self.half + to * self.big + start), size)
+
+    def give(self, name, rows, device):
+        self.net.put((self.tag,) + name, self.out.at[rows], self.out.at[rows], device)
+
+    def mirror(self, s, d):
+        if self.twin is not None:
+            rows = self.piece(s, d, 0, self.big)
+            self.net.put((self.tag, 6, s, d), self.out.at[rows], self.twin.at[rows], self.at.sib)
+
     def spread(self, s):
-        rows = pl.ds(up16(s * self.half + self.pos[s][0] * self.big), self.big)
         for k in range(1, 8):
             self.net.got((self.tag, 3, s, k))
-        for d in (1, 2, 3):
-            self.net.put((self.tag, 4, s, d), self.out.at[rows], self.out.at[rows], self.rings[s][0][d - 1])
-
-    def end(self):
+        for d in (1, 3):
+            self.give((4, s, d), self.piece(s, 0, 0, self.big), self.rings[s][0][d - 1])
+        self.mirror(s, 0)
+
+    def relay(self, s):
+        h = self.big // 2
+        for d, start in ((1, 0), (3, h)):
+            self.net.got((self.tag, 4, s, d))
+            self.give((5, s, d), self.piece(s, 4 - d, start, h), self.rings[s][0][d - 1])
+        for d in (1, 3):
+            self.mirror(s, d)
+
+    def end(self, s):
+        for d in (1, 3):
+            self.net.got((self.tag, 5, s, d))
+        self.mirror(s, 2)
+
+    def mirrored(self):
         for s in (0, 1):
-            for d in (1, 2, 3):
-                self.net.got((self.tag, 4, s, d))
+            for d in range(4):
+                self.net.got((self.tag, 6, s, d))
 
 
 def column_sum8(values):
@@ -138,32 +163,38 @@
 
 
 def layer_kernel(
-    length_ref, tokens, cotangent, qkv_ref, out_ref, up_ref, down_ref, qvb_in, ob_in, g1_in, h1_in, g2_in, h2_in,
+    length_ref, tokens, cotangent, qkv_in, out_in, up_in, down_in, qvb_in, ob_in, g1_in, h1_in, g2_in, h2_in,
     ub_in, db_in,
     lo_ref, ig_ref, om_ref, oa_ref, ob_ref,
     x_all, cot, normed1, n1, scale1, wown, qkvt, attt, probs, out_all, up_oth, down_oth,
     h1, n2, scale2, normed2, n2t, cott, hid, gpre, gn, gn_sib, mo, mo_sib, gh1, gb, acc, small, gattt, gt,
     g1_own, g1_sib, g1_sum, g1_far, gn1_keep, gn1_out, gn1_in, gn1_mine, gn1_far,
-    gm, ga, m1, mp1, m2, a1, ap1, a2, vec, vec_up, send, recv,
+    gm, ga, m1, mp1, m2, a1, ap1, a2, vec, vec_up, up_ref, down_ref, send, recv, near,
 ):
     at = Place()
     i, j = at.i, at.j
+    mine, theirs = pl.ds(up16(256 * j), 256), pl.ds(up16(256 * (1 - j)), 256)
+    ihalf = pl.ds(up16(384 * i), 384)
+    local = [(tokens, x_all.at[mine])]
+    local += [(qkv_in.at[t, pl.ds(up16(192 * j), 192)], wown.at[pl.ds(192 * t, 192)]) for t in range(3)]
+    local += [(cotangent, cot.at[mine]), (out_in, out_all.at[ihalf]), (up_in, up_ref), (down_in, down_ref)]
+    local = [pltpu.make_async_copy(src, dst, near.at[n]) for n, (src, dst) in enumerate(local)]
+    for copy in local:
+        copy.start()
     bar = pltpu.get_barrier_semaphore()
     peers = at.all()
     for peer in peers:
         pl.semaphore_signal(bar, inc=1, device_id=peer, device_id_type=MESH)
     pl.semaphore_wait(bar, len(peers))
     net = Copies(send, recv)
-    mine, theirs = pl.ds(up16(256 * j), 256), pl.ds(up16(256 * (1 - j)), 256)
     ipart, opart = cols128(384 * i, 384), cols128(384 * (1 - i), 384)
-    ihalf = pl.ds(up16(384 * i), 384)
 
     net.put("tok", tokens, x_all.at[mine], at.sib)
     net.put("cot", cotangent, cot.at[mine], at.sib)
     odd_y, odd_z = lax.rem(at.y, 2), lax.rem(at.z, 2)
     quarter = 2 * odd_y + odd_z
     across = (quarter + 2 - 4 * odd_y, quarter + 1 - 2 * odd_z)
-    weights = (("up", up_ref, up_oth), ("down", down_ref, down_oth))
+    weights = (("up", up_in, up_oth), ("down", down_in, down_oth))
 
     def weight_rows(q, start, size):
         return pl.ds(up16(96 * q + start), size)
@@ -174,7 +205,7 @@
             net.put((name, "x", n), src.at[rows], dst.at[rows], peer)
     for n, peer in enumerate((at.xa, at.xb)):
         part = 192 * j + 96 * n
-        net.put(("out", n), out_ref.at[pl.ds(up16(part), 96)], out_all.at[pl.ds(up16(384 * i + part), 96)], peer)
+        net.put(("out", n), out_in.at[pl.ds(up16(part), 96)], out_all.at[pl.ds(up16(384 * i + part), 96)], peer)
 
     def pass_on(which):
         name, _, dst = weights[which]
@@ -199,12 +230,6 @@
             net.got((name, axis, axis))
             for n in range(2):
                 net.got((name, "d", axis, n))
-
-    x_all[mine, :] = tokens[...]
-    cot[mine, :] = cotangent[...]
-    out_all[ihalf, :] = out_ref[...]
-    for t in range(3):
-        wown[pl.ds(192 * t, 192), :] = qkv_ref[t, pl.ds(up16(192 * j), 192), :]
 
     def first_norm(start):
         @pl.loop(0, 4)
@@ -222,9 +247,12 @@
         vec[n : n + 1, :] = ref[...].reshape(1, 768)
     vec[V_DB : V_DB + 1, 0:384] = db_in[...].reshape(1, 384)
     vec_up[...] = ub_in[...].reshape(1, 1536)
+    local[0].wait()
     first_norm(256 * j)
     net.got("tok")
     first_norm(256 * (1 - j))
+    for copy in local[1:4]:
+        copy.wait()
 
     ones = jnp.ones((16, 512), BF16)
     line = lax.broadcasted_iota(jnp.int32, (16, 192), 0)
@@ -267,6 +295,8 @@
 
     pass_on(1)
 
+    for copy in local[4:]:
+        copy.wait()
     net.got("cot")
     cott[...] = cot[:, ipart].T
     small[...] = jnp.zeros_like(small)
@@ -370,7 +400,7 @@
     put_small(S_OB, jnp.sum(acc[16:24, 0:768], axis=0, keepdims=True))
     put_small(S_UB, acc[24:25, :])
 
-    gattt[...] = dot(out_ref[pl.ds(up16(192 * j), 192), :], gb[...], 1, 1).astype(BF16)
+    gattt[...] = dot(out_all[pl.ds(up16(own_rows), 192), :], gb[...], 1, 1).astype(BF16)
     net.got("mo")
     lo_ref[...] = (lo_part + mo_sib[...]).astype(BF16)
 
@@ -438,7 +468,7 @@
     for c in range(6):
         ga[pl.ds(3456 + 192 * c, 192), :] = r[:, 128 * c : 128 * c + 128]
     ga[pl.ds(4608 + S_ROWS, 512 - S_ROWS), :] = jnp.zeros((512 - S_ROWS, 128), BF16)
-    tail = Reduce("a", net, at, ga, oa_ref, a1, ap1, a2)
+    tail = Reduce("a", net, at, ga, oa_ref, a1, ap1, a2, ob_ref)
     tail.start(0)
 
     net.got("g1x")
@@ -460,6 +490,10 @@
     big.spread(0)
     tail.spread(0)
     tail.spread(1)
+    big.relay(1)
+    big.relay(0)
+    tail.relay(0)
+    tail.relay(1)
     net.got("gn1x")
 
     @pl.loop(0, 4)
@@ -473,10 +507,10 @@
         mn = jnp.mean(e * n, axis=-1, keepdims=True)
         ig_ref[rows, :] = gh1[full, :] + (e - m - n * mn) * scale1[full, 0:1]
 
-    big.end()
-    tail.end()
-    net.put("sib", oa_ref, ob_ref, at.sib)
-    net.got("sib")
+    for reduce in (big, tail):
+        reduce.end(1)
+        reduce.end(0)
+    tail.mirrored()
     net.finish()
 
 
@@ -496,15 +530,15 @@
         V((9216, 128), BF16), V((5120, 128), BF16),
         V((2, 3, 1152, 128), BF16), V((2, 1152, 128), BF16), V((2, 7, 144, 128), BF16),
         V((2, 3, 640, 128), BF16), V((2, 640, 128), BF16), V((2, 7, 80, 128), BF16),
-        V((8, 768), F32), V((1, 1536), F32),
-        pltpu.SemaphoreType.DMA((160,)), pltpu.SemaphoreType.DMA((160,)),
+        V((8, 768), F32), V((1, 1536), F32), V((384, 1536), BF16), V((384, 1536), BF16),
+        pltpu.SemaphoreType.DMA((160,)), pltpu.SemaphoreType.DMA((160,)), pltpu.SemaphoreType.DMA((8,)),
     ]
     vm = pl.BlockSpec(memory_space=V)
     return pl.pallas_call(
         layer_kernel,
         out_shape=(sds((256, 384), BF16), sds((256, 768), F32), sds((9216, 128), BF16), sds((5120, 128), BF16),
                    sds((5120, 128), BF16)),
-        in_specs=[pl.BlockSpec(memory_space=pltpu.SMEM)] + [vm] * 14,
+        in_specs=[pl.BlockSpec(memory_space=pltpu.SMEM)] + [pl.BlockSpec(memory_space=pltpu.HBM)] * 6 + [vm] * 8,
         out_specs=(vm,) * 5,
         scratch_shapes=scratch,
         compiler_params=pltpu.CompilerParams(collective_id=0, has_side_effects=True, vmem_limit_bytes=60 << 20),
@@ -512,8 +546,8 @@
     )(*args)
 
 
-def finish_kernel(lo, ig, om_in, oa_in, ob_in, lo_out, ig_out, qkv_out, qvb_out, ow_out, out_bias, gain1, shift1, gain2, shift2,
-                  up_out, up_bias, down_out, down_bias, qkv, ow, up, down, om, oa, ob,
+def finish_kernel(lo_in, ig_in, om_in, oa_in, ob_in, lo_out, ig_out, qkv_out, qvb_out, ow_out, out_bias, gain1, shift1, gain2, shift2,
+                  up_out, up_bias, down_out, down_bias, qkv, ow, up, down, om, oa, ob, lo, ig,
                   sems, in_sems):
     j = lax.axis_index("grid")
     copies = []
@@ -521,7 +555,7 @@
     fetch = [
         pltpu.make_async_copy(src, dst, in_sems.at[n])
         for n, (src, dst) in enumerate(
-            [(om_in.at[h], om.at[h]) for h in halves] + [(oa_in, oa), (ob_in, ob)])
+            [(om_in.at[h], om.at[h]) for h in halves] + [(oa_in, oa), (ob_in, ob), (lo_in, lo), (ig_in, ig)])
     ]
     for copy in fetch:
         copy.start()
@@ -531,8 +565,6 @@
         copy.start()
         copies.append(copy)
 
-    send(lo, lo_out)
-    send(ig, ig_out)
     for s, scr, dst in ((0, up, up_out), (1, down, down_out)):
         fetch[s].wait()
         for c in range(12):
@@ -545,6 +577,10 @@
         for c in range(6):
             ow[rows, 128 * c : 128 * c + 128] = src[3456 + 192 * c : 3648 + 192 * c, :].astype(F32)
     send(ow, ow_out)
+    fetch[4].wait()
+    fetch[5].wait()
+    send(lo, lo_out)
+    send(ig, ig_out)
     for n in range(3):
         for src, side in ((oa, j), (ob, 1 - j)):
             rows = pl.ds(pl.multiple_of(192 * side, 192), 192)
@@ -576,8 +612,9 @@
         out_specs=(hbm, hbm, hbm, V, hbm, V, V, V, V, V, hbm, V, hbm, V),
         scratch_shapes=[pltpu.VMEM((3, 384, 768), F32), pltpu.VMEM((384, 768), F32), pltpu.VMEM((384, 1536), F32),
                         pltpu.VMEM((384, 1536), F32), pltpu.VMEM((9216, 128), BF16), pltpu.VMEM((5120, 128), BF16),
-                        pltpu.VMEM((5120, 128), BF16), pltpu.SemaphoreType.DMA((8,)), pltpu.SemaphoreType.DMA((4,))],
-        compiler_params=pltpu.CompilerParams(vmem_limit_bytes=40 << 20),
+                        pltpu.VMEM((5120, 128), BF16), pltpu.VMEM((256, 384), BF16), pltpu.VMEM((256, 768), F32),
+                        pltpu.SemaphoreType.DMA((8,)), pltpu.SemaphoreType.DMA((6,))],
+        compiler_params=pltpu.CompilerParams(vmem_limit_bytes=60 << 20),
         name="finish",
     )(*args)
 

time: 122 us -> 110 us (0.902)
  local copies, waits for them, and re-layouts: 6.35 us -> 0 us
  Pallas kernels: 114 us -> 108 us
    pallas_call x1, Pallas kernels: 109 us -> 102 us  [layer_call(): pl.pallas_call(layer_kernel, out_shape=(sds((256, 384), BF16), sds((256,...]
    unnamed x10 -> x0, local copies, waits for them, and re-layouts: 6.35 us -> none
where the time goes in v5:
time: 110 us
  Pallas kernels  108 us (98%)
  between operations  1.3 us (1%)
    pallas_call x1, Pallas kernels, layer_call(): pl.pallas_call(layer_kernel, out_shape=(sds((256, 384), BF16), sds((256,...  102 us
    pallas_call x1, Pallas kernels, finish(): pl.pallas_call(finish_kernel, out_shape=(jax.ShapeDtypeStruct((256, 384),...  6.24 us

profile of v5, /device:TPU:1, one launch (start us, length us, event | category | flops | bytes accessed | tf_op | source)
XLA Modules:
  0.0 109.7 jit_solution(13514688445685004366)
XLA Ops:
  1.3 102.1 %layer.1 = (bf16[256,384]{1,0:T(8,128)(2,1)}, f32[256,768]{1,0:T(8,128)}, bf16[9216,128]{1,0:T(8,128)(2,1)}, bf16[5120,128]{1,0:T(8,128)(2,1)}, bf16[5120,128]{1,0:T(8,128)(2,1)}) custom-call(s32[1]{0:T(128)S(6)} %copy.29.length_ref, bf16[256,768]{1,0:T(8,128)(2,1)} %tokens.1, bf16[256,768]{1,0:T(8,128)(2,1)} %cotangent.1, bf16[3,384,768]{2,1,0:T(8,128)(2,1)} %qkv_in.1, ...), custom_call_target="tpu_custom_call" | custom-call | tf_op jit(solution)/shard_map/layer/pallas_call | solution.py:537
  103.4 6.2 %finish.1 = (bf16[256,384]{1,0:T(8,128)(2,1)}, f32[256,768]{1,0:T(8,128)}, f32[3,384,768]{2,1,0:T(8,128)}, f32[2,384]{1,0:T(2,128)}, f32[384,768]{1,0:T(8,128)},...) custom-call(bf16[256,384]{1,0:T(8,128)(2,1)} %get-tuple-element.19.l, ...), custom_call_target="tpu_custom_call" | custom-call | tf_op jit(solution)/shard_map/finish/pallas_call | solution.py:607

commit v6 on v5

--- a/solution.py
+++ b/solution.py
@@ -41,6 +41,7 @@
             [8 * (lax.rem(self.z + d, 4) - self.z) for d in range(4)],
         )
         flip = [0, 1 - 2 * self.xh]
+        self.far = {"dp": dp + flip[1]}
         self.ring = [[{"dp": dp + r[d]} for d in (1, 2, 3)] for r in steps]
         self.eight = [[{"dp": dp + r[k // 2] + flip[k % 2]} for k in range(8)] for r in steps]
 
@@ -154,6 +155,60 @@
                 self.net.got((self.tag, 6, s, d))
 
 
+class Narrow(Reduce):
+    def __init__(self, tag, net, at, src, out, r1, p1, r2, p2, rx):
+        super().__init__(tag, net, at, src, out, r1, p1, r2)
+        self.p2, self.rx, self.small = p2, rx, self.half // 16
+        self.seconds = (at.ring[1], at.ring[0])
+
+    def second(self, s):
+        base = s * self.half + self.pos[s][0] * self.big
+        for d in (1, 2, 3):
+            self.net.got((self.tag, 1, s, d))
+        for d in (1, 2, 3, 0):
+            off = lax.rem(self.pos[s][1] + d, 4) * self.small
+            rows = pl.ds(up16(off), self.small)
+            total = self.src[pl.ds(up16(base + off), self.small), :].astype(F32)
+            for e in range(3):
+                total = total + self.r1[s, e, rows, :].astype(F32)
+            self.p1[s, rows, :] = total.astype(BF16)
+            if d:
+                self.net.put((self.tag, 2, s, d), self.p1.at[s, rows], self.r2.at[s, d - 1], self.seconds[s][d - 1])
+
+    def third(self):
+        for s in (0, 1):
+            for d in (1, 2, 3):
+                self.net.got((self.tag, 2, s, d))
+            total = self.p1[s, pl.ds(up16(self.pos[s][1] * self.small), self.small), :].astype(F32)
+            for e in range(3):
+                total = total + self.r2[s, e].astype(F32)
+            self.p2[s] = total.astype(BF16)
+        self.net.put((self.tag, 7), self.p2.at[1 - self.at.xh], self.rx, self.at.far)
+
+    def start_of(self, s):
+        return s * self.half + self.pos[s][0] * self.big + self.pos[s][1] * self.small
+
+    def middle(self):
+        self.net.got((self.tag, 7))
+        where = self.start_of(0) + self.at.xh * (self.start_of(1) - self.start_of(0))
+        rows = pl.ds(up16(where), self.small)
+        self.out[rows, :] = (self.p2[self.at.xh].astype(F32) + self.rx[...].astype(F32)).astype(BF16)
+        self.give((8,), rows, self.at.far)
+
+    def back(self):
+        self.net.got((self.tag, 8))
+        for s in (0, 1):
+            rows = pl.ds(up16(self.start_of(s)), self.small)
+            for d in (1, 2, 3):
+                self.give((3, s, d), rows, self.seconds[s][d - 1])
+
+    def spread(self, s):
+        for d in (1, 2, 3):
+            self.net.got((self.tag, 3, s, d))
+        for d in (1, 3):
+            self.give((4, s, d), self.piece(s, 0, 0, self.big), self.rings[s][0][d - 1])
+
+
 def column_sum8(values):
     return jnp.sum(values.reshape(values.shape[0] // 8, 8, values.shape[1]), axis=0)
 
@@ -169,7 +224,7 @@
     x_all, cot, normed1, n1, scale1, wown, qkvt, attt, probs, out_all, up_oth, down_oth,
     h1, n2, scale2, normed2, n2t, cott, hid, gpre, gn, gn_sib, mo, mo_sib, gh1, gb, acc, small, gattt, gt,
     g1_own, g1_sib, g1_sum, g1_far, gn1_keep, gn1_out, gn1_in, gn1_mine, gn1_far,
-    gm, ga, m1, mp1, m2, a1, ap1, a2, vec, vec_up, up_ref, down_ref, send, recv, near,
+    gm, ga, m1, mp1, m2, mp2, mx, a1, ap1, a2, vec, vec_up, up_ref, down_ref, send, recv, near,
 ):
     at = Place()
     i, j = at.i, at.j
@@ -362,7 +417,7 @@
         gn[rows, opart] = dot(gpre[rows, :], up_oth[...], 1, 1).astype(BF16)
         net.put(("gn", c), gn.at[rows], gn_sib.at[rows], at.sib)
 
-    big = Reduce("m", net, at, gm, om_ref, m1, mp1, m2)
+    big = Narrow("m", net, at, gm, om_ref, m1, mp1, m2, mp2, mx)
     for s, left, right in ((1, cott, hid), (0, n2t, gpre)):
         @pl.loop(0, 6)
         def _(c):
@@ -481,19 +536,20 @@
     big.second(0)
     tail.second(0)
     tail.second(1)
-    big.own(1)
-    big.own(0)
+    big.third()
     tail.own(0)
     tail.own(1)
+    big.middle()
+    big.back()
     net.put("gn1x", gn1_mine, gn1_far, at.xa)
+    tail.spread(0)
+    tail.spread(1)
     big.spread(1)
     big.spread(0)
-    tail.spread(0)
-    tail.spread(1)
+    tail.relay(0)
+    tail.relay(1)
     big.relay(1)
     big.relay(0)
-    tail.relay(0)
-    tail.relay(1)
     net.got("gn1x")
 
     @pl.loop(0, 4)
@@ -507,7 +563,7 @@
         mn = jnp.mean(e * n, axis=-1, keepdims=True)
         ig_ref[rows, :] = gh1[full, :] + (e - m - n * mn) * scale1[full, 0:1]
 
-    for reduce in (big, tail):
+    for reduce in (tail, big):
         reduce.end(1)
         reduce.end(0)
     tail.mirrored()
@@ -528,7 +584,8 @@
         V((16, 768), F32), V((16, 768), F32), V((16, 768), F32), V((16, 768), F32),
         V((512, 768), F32), V((256, 768), BF16), V((256, 768), BF16), V((256, 768), BF16), V((256, 768), BF16),
         V((9216, 128), BF16), V((5120, 128), BF16),
-        V((2, 3, 1152, 128), BF16), V((2, 1152, 128), BF16), V((2, 7, 144, 128), BF16),
+        V((2, 3, 1152, 128), BF16), V((2, 1152, 128), BF16), V((2, 3, 288, 128), BF16),
+        V((2, 288, 128), BF16), V((288, 128), BF16),
         V((2, 3, 640, 128), BF16), V((2, 640, 128), BF16), V((2, 7, 80, 128), BF16),
         V((8, 768), F32), V((1, 1536), F32), V((384, 1536), BF16), V((384, 1536), BF16),
         pltpu.SemaphoreType.DMA((160,)), pltpu.SemaphoreType.DMA((160,)), pltpu.SemaphoreType.DMA((8,)),

time: 110 us -> 109 us (level)
    pallas_call x1, Pallas kernels: 102 us -> 101 us  [layer_call(): pl.pallas_call(layer_kernel, out_shape=(sds((256, 384), BF16), sds((256,...]
where the time goes in v6:
time: 109 us; the launch traced here: 108 us
  Pallas kernels  107 us (98%)
  between operations  1.3 us (1%)
    pallas_call x1, Pallas kernels, layer_call(): pl.pallas_call(layer_kernel, out_shape=(sds((256, 384), BF16), sds((256,...  101 us
    pallas_call x1, Pallas kernels, finish(): pl.pallas_call(finish_kernel, out_shape=(jax.ShapeDtypeStruct((256, 384),...  6.24 us

profile of v6, /device:TPU:1, one launch (start us, length us, event | category | flops | bytes accessed | tf_op | source)
XLA Modules:
  0.0 108.5 jit_solution(14202044102015647684)
XLA Ops:
  1.3 100.9 %layer.1 = (bf16[256,384]{1,0:T(8,128)(2,1)}, f32[256,768]{1,0:T(8,128)}, bf16[9216,128]{1,0:T(8,128)(2,1)}, bf16[5120,128]{1,0:T(8,128)(2,1)}, bf16[5120,128]{1,0:T(8,128)(2,1)}) custom-call(s32[1]{0:T(128)S(6)} %copy.29.length_ref, bf16[256,768]{1,0:T(8,128)(2,1)} %tokens.1, bf16[256,768]{1,0:T(8,128)(2,1)} %cotangent.1, bf16[3,384,768]{2,1,0:T(8,128)(2,1)} %qkv_in.1, ...), custom_call_target="tpu_custom_call" | custom-call | tf_op jit(solution)/shard_map/layer/pallas_call | solution.py:594
  102.2 6.2 %finish.1 = (bf16[256,384]{1,0:T(8,128)(2,1)}, f32[256,768]{1,0:T(8,128)}, f32[3,384,768]{2,1,0:T(8,128)}, f32[2,384]{1,0:T(2,128)}, f32[384,768]{1,0:T(8,128)},...) custom-call(bf16[256,384]{1,0:T(8,128)(2,1)} %get-tuple-element.19.l, ...), custom_call_target="tpu_custom_call" | custom-call | tf_op jit(solution)/shard_map/finish/pallas_call | solution.py:664
